TPU v7x, 32 devices: a whole 2x2x4 slice. The times are simulated.
32 devices in a mesh: dp: 2 (over core), row: 4 (over y, x), col: 4 (over z).
Axes of the slice: x: 2, y: 2, z: 4, core: 2. Of those that a mesh axis runs over, the one named last changes fastest.
Arguments:
- block_input: float32 [768, 10240], P('row', ('dp', 'col')), may hold values from -32 to 32
- segment_ids: int32 [10240], replicated, may hold values from 0 to 12, as said below
- parent_ids: int32 [13], replicated, may hold values from 0 to 12, as said below
- attn_gain: float32 [768], P('row'), may hold values from 0.5 to 1.5
- attn_shift: float32 [768], P('row'), may hold values from -1.25 to 1.25
- qkv_weight: float32 [3, 12, 49152], P(None, 'col', 'row'), may hold values from -0.3125 to 0.3125
- qkv_bias: float32 [3, 768], P(None, 'col'), may hold values from -1.25 to 1.25
- proj_weight: float32 [12, 49152], P('col', 'row'), may hold values from -1.5 to 1.5
- proj_bias: float32 [768], P('row'), may hold values from -1.25 to 1.25
- mlp_gain: float32 [768], P('row'), may hold values from 0.5 to 1.5
- mlp_shift: float32 [768], P('row'), may hold values from -1.25 to 1.25
- up_weight: float32 [768, 3072], P('row', 'col'), may hold values from -0.21875 to 0.21875
- up_bias: float32 [3072], P('col'), may hold values from -1.25 to 1.25
- down_weight: float32 [768, 3072], P('row', 'col'), may hold values from -0.109375 to 0.109375
- down_bias: float32 [768], P('row'), may hold values from -1.25 to 1.25
- cotangent: float32 [768, 10240], P('row', ('dp', 'col')), may hold values from -6 to 6
Outputs:
- block_output: float32 [768, 10240], P('row', ('dp', 'col'))
- input_grad: float32 [768, 10240], P('row', ('dp', 'col'))
- attn_gain_grad: float32 [768], P('row')
- attn_shift_grad: float32 [768], P('row')
- qkv_weight_grad: float32 [3, 12, 49152], P(None, 'col', 'row')
- qkv_bias_grad: float32 [3, 768], P(None, 'col')
- proj_weight_grad: float32 [12, 49152], P('col', 'row')
- proj_bias_grad: float32 [768], P('row')
- mlp_gain_grad: float32 [768], P('row')
- mlp_shift_grad: float32 [768], P('row')
- up_weight_grad: float32 [768, 3072], P('row', 'col')
- up_bias_grad: float32 [3072], P('col')
- down_weight_grad: float32 [768, 3072], P('row', 'col')
- down_bias_grad: float32 [768], P('row')
Inputs may be any that keep to these rules, and one draw needn't show every extreme that they name: `segment_ids`: rows split into trees of 10240 consecutive tokens from row 0. A tree has 13 segments, each a run of consecutive tokens: the trunk first (a quarter to a half of the tree), then each of the 4 branches followed by its 2 leaves. Every id names one segment of one tree; tree t holds the ids t * 13 to t * 13 + 12, its trunk the last of them and its first branch the first. `parent_ids`: A branch's parent is its tree's trunk, a leaf's parent its branch; a trunk is its own parent.
All inputs are finite; a program needn't handle non-finite values.
Results may differ from a plain program's by a relative error of at most 0.013.
The roundings to bfloat16 on the way count: a program that leaves them out, or rounds other values in their place, can miss the bound.
Values may be sent and summed in bfloat16 or wider, within the bound.
No kernel may reach another device: no remote copies, remote signals or barrier semaphores. Data moves between devices by JAX's collectives and lax.ppermute only.
A program may use at most 192 MiB of HBM per device.

v0:
```python
import functools

import jax
import jax.numpy as jnp
from jax import lax
from jax.experimental import pallas as pl
from jax.experimental.pallas import tpu as pltpu
from jax.sharding import PartitionSpec as P

HEAD_DIM = 64
LOG2E = 1.4426950408889634
BIG = 2.0**126
FLOOR = -1e30
KEY_BLOCK = 512
KEY_BLOCK_BACK = 512
SUB_BLOCK = 128
AHEAD = 2
VMEM_BYTES = 56 * 1024 * 1024


def sign_low(s):
    scaled = s.astype(jnp.bfloat16) * jnp.bfloat16(BIG)
    return jnp.minimum(jnp.maximum(scaled, jnp.bfloat16(-1)), jnp.bfloat16(1))


def matmul(a, b, left=1):
    return lax.dot_general(a, b, (((left,), (0,)), ((), ())), preferred_element_type=jnp.float32)


def start_parts(offs, parts, held, sem, rows):
    chunks = parts[0].shape[1] // rows
    for p, part in enumerate(parts):
        for c in range(chunks):
            start = pl.multiple_of(offs[p * chunks + c], rows)
            pltpu.make_async_copy(
                part.at[:, pl.ds(c * rows, rows), :], held.at[:, pl.ds(start, rows), :], sem.at[p]
            ).start()


def wait_parts(parts, held, sem):
    for p, part in enumerate(parts):
        pltpu.make_async_copy(part, held.at[:, pl.ds(0, part.shape[1]), :], sem.at[p]).wait()


def lower(acc, held, first, count):
    for h in range(held.shape[0]):
        held[h, pl.ds(first, count), :] = acc[h, pl.ds(first, count), :].astype(jnp.bfloat16)


def store_grads(acc, held, grads, sem):
    if len(grads.shape) == 3:
        lower(acc, held, 0, held.shape[1])
        pltpu.make_async_copy(held, grads, sem).start()
    else:
        groups, _, cols, pair, rows, _ = grads.shape
        for e in range(pair):
            for c in range(cols):
                first = (e * cols + c) * groups * rows
                lower(acc, held, first, groups * rows)
                for r in range(groups):
                    pltpu.make_async_copy(
                        held.at[:, pl.ds(first + r * rows, rows), :],
                        grads.at[r, :, c, e, :, :],
                        sem,
                    ).start()
    pltpu.make_async_copy(held, held, sem).wait()


def visible(keys, anc, pos, start, block, queries):
    repeat = -(-queries // 128)
    codes = jnp.concatenate([keys[pl.ds(start, block), :]] * repeat, axis=1)[:, :queries]
    return ((codes & anc) != 0) & (codes <= pos)


def fill_keys(code, keys):
    def fill(i, carry):
        at = pl.multiple_of(i * 128, 128)
        keys[pl.ds(at, 128), :] = jnp.broadcast_to(code[:, pl.ds(at, 128)], (128, 128)).T
        return carry

    lax.fori_loop(0, keys.shape[0] // 128, fill, 0, unroll=8)


def turn(block):
    return block.astype(jnp.float32).T


def sweep(counts, lists, b, key_block, step):
    full, some = counts[b, 0], counts[b, 1]

    def start(i):
        return pl.multiple_of(lists[b, i] * key_block, key_block)

    def plain(i, carry):
        step(start(i), False)
        return carry

    def masked(i, carry):
        step(start(i), True)
        return carry

    lax.fori_loop(0, full, plain, 0)
    lax.fori_loop(full, some, masked, 0)


def shuffle(source, target, order, rows, first=0):
    for place, origin in enumerate(order):
        at = first + place * rows
        target[at : at + rows, :] = source[origin * rows : (origin + 1) * rows, :]


def unshuffle(source, target, order, rows, first=0):
    for place, origin in enumerate(order):
        part = source[first + place * rows : first + (place + 1) * rows, :]
        part = part[:, : target.shape[1]].astype(target.dtype)
        target[origin * rows : (origin + 1) * rows, :] = part


def forward_kernel(
    heads,
    part_count,
    rows,
    order,
    order_rows,
    block,
    cnt,
    lst,
    offs,
    q_ref,
    code,
    anc_ref,
    pos_ref,
    *rest,
):
    parts = rest[:part_count]
    o_ref, low_ref, qs, os, held, right, acc, top, keys, sem = rest[part_count:]
    b = pl.program_id(0)
    width = heads * HEAD_DIM

    @pl.when(b == 0)
    def _():
        start_parts(offs, parts, held, sem, rows)
        right[...] = jnp.zeros_like(right)
        shuffle(q_ref, qs, order, order_rows)
        fill_keys(code, keys)
        wait_parts(parts, held, sem)

    acc[...] = jnp.zeros_like(acc)
    top[...] = jnp.full_like(top, FLOOR)
    at = pl.multiple_of(b * block, block)
    turned = turn(qs[pl.ds(at, block), :]).astype(jnp.bfloat16)
    for h in range(heads):
        right[h, 0:HEAD_DIM, :] = turned[h * HEAD_DIM : (h + 1) * HEAD_DIM]

    def step(start, masked):
        mask = None
        if masked:
            mask = visible(keys, anc_ref[...], pos_ref[...], start, KEY_BLOCK, block)
        scores = [matmul(held[h, pl.ds(start, KEY_BLOCK), :], right[h]) for h in range(heads)]
        signed, scales, sums = [], [], []
        for h in range(heads):
            s = scores[h]
            size = jnp.abs(s * LOG2E)
            if masked:
                size = jnp.where(mask, size, FLOOR)
            old = top[h]
            new = jnp.maximum(old, jnp.max(size, axis=0, keepdims=True))
            e = jnp.exp2(size - new)
            signed.append(e.astype(jnp.bfloat16) * sign_low(s))
            scales.append(jnp.exp2(old - new))
            top[h] = new
            sums.append(jnp.sum(e, axis=0, keepdims=True))
        for h in range(heads):
            out = matmul(held[h, pl.ds(start, KEY_BLOCK), HEAD_DIM:], signed[h], 0)
            acc[h, 0:HEAD_DIM, :] = acc[h, 0:HEAD_DIM, :] * scales[h] + out
            acc[h, HEAD_DIM : HEAD_DIM + 1, :] = (
                acc[h, HEAD_DIM : HEAD_DIM + 1, :] * scales[h] + sums[h]
            )

    sweep(cnt, lst, b, KEY_BLOCK, step)
    outs, logs = [], []
    for h in range(heads):
        weight = acc[h, HEAD_DIM : HEAD_DIM + 1, :]
        outs.append(acc[h, 0:HEAD_DIM, :] / weight)
        logs.append(top[h] + jnp.log2(weight))
    fill = jnp.zeros((os.shape[1] - width - heads, block), jnp.float32)
    os[pl.ds(at, block), :] = jnp.concatenate(outs + logs + [fill], axis=0).T

    @pl.when(b == pl.num_programs(0) - 1)
    def _():
        unshuffle(os, o_ref, order, order_rows)
        unshuffle(os, low_ref, order, order_rows)


def query_block(count, whole_count=None):
    return 256 if count % 256 == 0 else whole_count or count


def whole(shape):
    return pl.BlockSpec(shape, lambda b, *_: (0,) * len(shape))


def lanes(size):
    return pl.BlockSpec((1, size), lambda b, *_: (0, b))


def stat_width(heads):
    return -(-(heads * HEAD_DIM + heads) // 128) * 128


def work(passes, count, all_keys, heads):
    return pl.CostEstimate(
        flops=2 * passes * count * all_keys * 256 * heads,
        bytes_accessed=4 * heads * all_keys * 2 * HEAD_DIM,
        transcendentals=count * all_keys * heads,
    )


def attend_forward(cnt, lst, offs, q, code, anc, pos, parts, rows, order, order_rows):
    count, width = q.shape
    heads = width // HEAD_DIM
    all_keys = code.shape[1]
    block = query_block(count)
    part_count = len(parts)
    full = stat_width(heads)
    return pl.pallas_call(
        functools.partial(forward_kernel, heads, part_count, rows, order, order_rows, block),
        out_shape=(
            jax.ShapeDtypeStruct((count, full), jnp.float32),
            jax.ShapeDtypeStruct((count, width), jnp.bfloat16),
        ),
        grid_spec=pltpu.PrefetchScalarGridSpec(
            num_scalar_prefetch=3,
            grid=(count // block,),
            in_specs=[whole((count, width)), whole((1, all_keys)), lanes(block), lanes(block)]
            + [pl.BlockSpec(memory_space=pl.ANY)] * part_count,
            out_specs=[whole((count, full)), whole((count, width))],
            scratch_shapes=[
                pltpu.VMEM((count, width), jnp.bfloat16),
                pltpu.VMEM((count, full), jnp.float32),
                pltpu.VMEM((heads, all_keys, 2 * HEAD_DIM), jnp.bfloat16),
                pltpu.VMEM((heads, 2 * HEAD_DIM, block), jnp.bfloat16),
                pltpu.VMEM((heads, HEAD_DIM + 8, block), jnp.float32),
                pltpu.VMEM((heads, 1, block), jnp.float32),
                pltpu.VMEM((all_keys, 128), jnp.int32),
                pltpu.SemaphoreType.DMA((part_count,)),
            ],
        ),
        compiler_params=pltpu.CompilerParams(vmem_limit_bytes=VMEM_BYTES),
        cost_estimate=work(4, count, all_keys, heads),
    )(cnt, lst, offs, q, code, anc, pos, *parts)


def backward_kernel(
    heads,
    part_count,
    rows,
    order,
    order_rows,
    block,
    cnt,
    lst,
    offs,
    q_own,
    q_other,
    g_own,
    g_other,
    o_own,
    o_other,
    code,
    anc_ref,
    pos_ref,
    *rest,
):
    parts, (dq_own, dq_other, grads) = rest[:part_count], rest[part_count : part_count + 3]
    qs, gs, os, held, right, left, acc, dqs, dsum, stat, keys, sem, out_sem = rest[part_count + 3 :]
    b = pl.program_id(0)
    width = heads * HEAD_DIM

    @pl.when(b == 0)
    def _():
        start_parts(offs, parts, held, sem, rows)
        left[...] = jnp.zeros_like(left)
        right[...] = jnp.zeros_like(right)
        acc[...] = jnp.zeros_like(acc)
        shuffle(q_own, qs, order, order_rows)
        shuffle(q_other, qs, order, order_rows, q_own.shape[0])
        shuffle(g_own, gs, order, order_rows)
        shuffle(g_other, gs, order, order_rows, q_own.shape[0])
        shuffle(o_own, os, order, order_rows)
        shuffle(o_other, os, order, order_rows, q_own.shape[0])
        fill_keys(code, keys)
        wait_parts(parts, held, sem)

    dqs[...] = jnp.zeros_like(dqs)
    at = pl.multiple_of(b * block, block)
    q, g = qs[pl.ds(at, block), :], gs[pl.ds(at, block), :]
    turned_o = os[pl.ds(at, block), :].T
    turned_q = turn(q).astype(jnp.bfloat16)
    turned_g = turn(g)
    for h in range(heads):
        span = slice(h * HEAD_DIM, (h + 1) * HEAD_DIM)
        left[h, 0:block, 0:HEAD_DIM] = q[:, span]
        left[h, block:, HEAD_DIM:] = g[:, span]
        right[h, 0:HEAD_DIM, 0:block] = turned_q[span]
        right[h, HEAD_DIM:, block:] = turned_g[span].astype(jnp.bfloat16)
        stat[h : h + 1, :] = turned_o[width + h : width + h + 1]
        stat[8 + h : 9 + h, :] = jnp.sum(turned_g[span] * turned_o[span], axis=0, keepdims=True)

    def step(start, masked):
        mask = None
        if masked:
            mask = visible(keys, anc_ref[...], pos_ref[...], start, KEY_BLOCK_BACK, block)
        units = [(h, at) for at in range(0, KEY_BLOCK_BACK, SUB_BLOCK) for h in range(heads)]

        def scores(h, at):
            both = matmul(held[h, pl.ds(start + at, SUB_BLOCK), :], right[h])
            return both[:, :block], both[:, block:]

        def gradients(h, at, s, dp):
            e = jnp.exp2(jnp.abs(s * LOG2E) - stat[h : h + 1, :])
            if masked:
                e = jnp.where(mask[at : at + SUB_BLOCK], e, 0.0)
            sign = sign_low(s)
            signed = e.astype(jnp.bfloat16) * sign
            delta = stat[8 + h : 9 + h, :]
            ds = (e * (dp - sign.astype(jnp.float32) * delta)).astype(jnp.bfloat16)
            return ds, signed

        def gather_up(h, at, ds, signed):
            spot = pl.ds(start + at, SUB_BLOCK)
            acc[h, spot, :] += matmul(jnp.concatenate([ds, signed], axis=1), left[h])
            dqs[h] += matmul(held[h, spot, 0:HEAD_DIM], ds, 0)

        ready = [scores(*unit) for unit in units[:AHEAD]]
        last = None
        for i, unit in enumerate(units):
            if i + AHEAD < len(units):
                ready.append(scores(*units[i + AHEAD]))
            pair = gradients(*unit, *ready[i])
            if last is not None:
                gather_up(*last)
            last = unit + pair
        gather_up(*last)

    sweep(cnt, lst, b, KEY_BLOCK_BACK, step)
    fill = jnp.zeros((dsum.shape[1] - width, block), jnp.float32)
    dsum[pl.ds(at, block), :] = (
        jnp.concatenate([dqs[h] for h in range(heads)] + [fill], axis=0).T * 0.125
    )

    @pl.when(b == pl.num_programs(0) - 1)
    def _():
        store_grads(acc, held, grads, out_sem)
        unshuffle(dsum, dq_own, order, order_rows)
        unshuffle(dsum, dq_other, order, order_rows, q_own.shape[0])


def attend_backward(
    cnt, lst, offs, q, g, o, code, anc, pos, parts, rows, order, order_rows, grad_shape
):
    own, width = q[0].shape
    count = 2 * own
    heads = width // HEAD_DIM
    all_keys = code.shape[1]
    block = query_block(own, count)
    part_count = len(parts)
    full = o[0].shape[1]
    return pl.pallas_call(
        functools.partial(backward_kernel, heads, part_count, rows, order, order_rows, block),
        out_shape=(
            jax.ShapeDtypeStruct((own, full), jnp.float32),
            jax.ShapeDtypeStruct((own, full), jnp.float32),
            jax.ShapeDtypeStruct(grad_shape, jnp.bfloat16),
        ),
        grid_spec=pltpu.PrefetchScalarGridSpec(
            num_scalar_prefetch=3,
            grid=(count // block,),
            in_specs=[
                whole((own, width)),
                whole((own, width)),
                whole((own, width)),
                whole((own, width)),
                whole((own, full)),
                whole((own, full)),
                whole((1, all_keys)),
                lanes(block),
                lanes(block),
            ]
            + [pl.BlockSpec(memory_space=pl.ANY)] * part_count,
            out_specs=[whole((own, full)), whole((own, full)), pl.BlockSpec(memory_space=pl.ANY)],
            scratch_shapes=[
                pltpu.VMEM((count, width), jnp.bfloat16),
                pltpu.VMEM((count, width), jnp.bfloat16),
                pltpu.VMEM((count, full), jnp.float32),
                pltpu.VMEM((heads, all_keys, 2 * HEAD_DIM), jnp.bfloat16),
                pltpu.VMEM((heads, 2 * HEAD_DIM, 2 * block), jnp.bfloat16),
                pltpu.VMEM((heads, 2 * block, 2 * HEAD_DIM), jnp.bfloat16),
                pltpu.VMEM((heads, all_keys, 2 * HEAD_DIM), jnp.float32),
                pltpu.VMEM((heads, HEAD_DIM, block), jnp.float32),
                pltpu.VMEM((count, full), jnp.float32),
                pltpu.VMEM((16, block), jnp.float32),
                pltpu.VMEM((all_keys, 128), jnp.int32),
                pltpu.SemaphoreType.DMA((part_count,)),
                pltpu.SemaphoreType.DMA,
            ],
        ),
        compiler_params=pltpu.CompilerParams(vmem_limit_bytes=VMEM_BYTES),
        cost_estimate=work(5, count, all_keys, heads),
    )(cnt, lst, offs, *q, *g, *o, code, anc, pos, *parts)


def swap(value, axis, step):
    count = lax.axis_size(axis)
    return lax.ppermute(value, axis, [(source, source ^ step) for source in range(count)])


def exchange(pieces, axis):
    return [pieces[0]] + [swap(pieces[step], axis, step) for step in range(1, len(pieces))]


def gather(value, axis):
    return exchange([value] * lax.axis_size(axis), axis)


def after(value, *others):
    return lax.optimization_barrier((value,) + others)[0]


def pick(values, index, axis=0):
    return lax.dynamic_index_in_dim(values, index, axis, keepdims=False)


def reorder(pieces, index):
    stacked = jnp.stack(pieces)
    return jnp.stack([pick(stacked, index ^ place) for place in range(len(pieces))])


def total(pieces):
    result = pieces[0].astype(jnp.float32)
    for piece in pieces[1:]:
        result = result + piece.astype(jnp.float32)
    return result


def low(value):
    return value.astype(jnp.bfloat16)


def dot(left, right, left_dim=1, right_dim=0):
    return lax.dot_general(
        left, right, (((left_dim,), (right_dim,)), ((), ())), preferred_element_type=jnp.float32
    )


def trade(values, axis):
    return lax.all_to_all(values, axis, 0, 0)


def share(value, axis):
    return trade(jnp.broadcast_to(value[None], (lax.axis_size(axis),) + value.shape), axis)


def spread(columns, extra, cores, rows):
    features, tokens = columns.shape
    piece = tokens // (cores * rows)
    turned = columns.reshape(features, cores * rows, piece).transpose(1, 2, 0)
    if extra is not None:
        fill = jnp.broadcast_to(extra[None], (cores * rows,) + extra.shape)
        turned = jnp.concatenate([turned, fill], axis=1)
    got = trade(turned, ("dp", "row")).reshape(cores, rows, -1, features)
    held = got[:, :, :piece].transpose(0, 2, 1, 3).reshape(cores * piece, rows * features)
    if extra is None:
        return held
    return held, got[0, :, piece:].transpose(1, 0, 2).reshape(-1, rows * features)


def by_device(values, cores, rows):
    features = values.shape[1] // rows
    sent = values.reshape(cores, -1, rows, features).transpose(0, 2, 1, 3)
    return sent.reshape(cores * rows, -1, features)


def collect(first, second, extra, cores, rows):
    second = by_device(second, cores, rows)
    _, piece, features = second.shape
    sent = jnp.concatenate([first, second], axis=2)
    lines = extra.reshape(-1, 2, rows, features).transpose(2, 0, 1, 3).reshape(rows, -1, 2 * features)
    lines = jnp.pad(lines, ((0, 0), (0, 16 - lines.shape[1]), (0, 0)))
    lines = jnp.broadcast_to(lines[None], (cores,) + lines.shape)
    lines = lines.reshape((cores * rows,) + lines.shape[2:])
    got = trade(jnp.concatenate([sent, lines], axis=1), ("dp", "row"))
    turned = got[:, :piece].transpose(2, 0, 1).reshape(2, features, -1).astype(jnp.float32)
    sums = jnp.sum(got[:, piece:].astype(jnp.float32), axis=0)
    return turned[0], turned[1], sums


def norm_forward(inputs, gain, shift):
    average = jnp.mean(inputs, axis=1, keepdims=True)
    squares = jnp.mean(inputs * inputs, axis=1, keepdims=True)
    spread_rows = lax.rsqrt(squares - average * average + 1e-05)
    unit = (inputs - average) * spread_rows
    return low(unit * gain + shift), unit, spread_rows


def norm_backward(grad, unit, spread_rows, gain):
    scaled = grad * gain
    return spread_rows * (
        scaled
        - jnp.mean(scaled, axis=1, keepdims=True)
        - unit * jnp.mean(scaled * unit, axis=1, keepdims=True)
    )


def gelu_tanh(hidden):
    return jax.nn.gelu(hidden, approximate=True)


def everywhere(value, axis):
    return total(gather(value, axis))


def side_by_side(pieces):
    return pieces.transpose(1, 0, 2).reshape(pieces.shape[1], -1)


def three_low(value):
    first = low(value)
    second = low(value - first.astype(jnp.float32))
    third = low(value - first.astype(jnp.float32) - second.astype(jnp.float32))
    return jnp.stack([first, second, third])


def block_lists(hot, places, anc, pos, key_block, query_rows):
    def reduce(values, size, start, op):
        return lax.reduce(values.reshape(-1, size), jnp.int32(start), op, (1,))

    keys = hot.shape[0] // key_block
    key_or = reduce(hot, key_block, 0, lax.bitwise_or)[None]
    start = jnp.min(places.reshape(-1, key_block), axis=1)[None]
    end = jnp.max(places.reshape(-1, key_block), axis=1)[None]
    anc_or = reduce(anc, query_rows, 0, lax.bitwise_or)[:, None]
    anc_and = reduce(anc, query_rows, -1, lax.bitwise_and)[:, None]
    first = jnp.min(pos.reshape(-1, query_rows), axis=1)[:, None]
    last = jnp.max(pos.reshape(-1, query_rows), axis=1)[:, None]
    full = ((key_or & ~anc_and) == 0) & (end <= first)
    some = (((key_or & anc_or) != 0) & (start <= last)) | full
    numbers = jnp.arange(keys, dtype=jnp.int32)
    code = jnp.where(full, 0, jnp.where(some, 1, 2)) * keys + numbers[None]
    rank = jnp.sum((code[:, None, :] < code[:, :, None]).astype(jnp.int32), axis=2)
    order = jnp.sum(
        jnp.where(rank[:, None, :] == numbers[None, :, None], numbers[None, None], 0), axis=2
    )
    counts = jnp.stack(
        [jnp.sum(full.astype(jnp.int32), axis=1), jnp.sum(some.astype(jnp.int32), axis=1)], axis=1
    )
    return counts.astype(jnp.int32), order.astype(jnp.int32)


def shards(
    block_input,
    segment_ids,
    parent_ids,
    attn_gain,
    attn_shift,
    qkv_weight,
    qkv_bias,
    proj_weight,
    proj_bias,
    mlp_gain,
    mlp_shift,
    up_weight,
    up_bias,
    down_weight,
    down_bias,
    cotangent,
):
    cores, rows, cols = lax.axis_size("dp"), lax.axis_size("row"), lax.axis_size("col")
    core, row, col = lax.axis_index("dp"), lax.axis_index("row"), lax.axis_index("col")
    features, tokens = block_input.shape
    half = tokens // cores
    piece = half // rows
    own = cores * piece
    width_all = rows * features
    heads = qkv_weight.shape[1]
    width = heads * HEAD_DIM
    head_width = 2 * HEAD_DIM
    hidden_part = up_weight.shape[1] // cores
    head_part = width // cores
    segments = parent_ids.shape[0]
    queries = cols * own
    block_rows = query_block(queries)
    whole_chunks = piece % 16 == 0

    vectors = jnp.stack([attn_gain, attn_shift, mlp_gain, mlp_shift, proj_bias, down_bias])
    vectors = jnp.pad(vectors, ((0, 2), (0, 0)))
    layer_in, vectors = spread(block_input, vectors, cores, rows)

    packed = low(qkv_weight).reshape(3, heads, features, HEAD_DIM)
    qkv_low = jnp.concatenate(
        [packed[kind, h] for h in range(heads) for kind in (1, 2)]
        + [packed[0, h] for h in range(heads)],
        axis=1,
    )
    bias = qkv_bias.reshape(3, heads, HEAD_DIM)
    bias_row = jnp.concatenate(
        [bias[kind, h] for h in range(heads) for kind in (1, 2)] + [bias[0].reshape(-1)]
    )

    proj_low = (
        low(proj_weight).reshape(heads, features, HEAD_DIM).transpose(0, 2, 1)
    ).reshape(width, features)
    up_low, down_low = [
        lax.dynamic_slice_in_dim(low(w), core * hidden_part, hidden_part, 1)
        for w in (up_weight, down_weight)
    ]
    up_bias_part = three_low(lax.dynamic_slice_in_dim(up_bias, core * hidden_part, hidden_part, 0))
    bias_rows = jnp.pad(up_bias_part, ((0, 13), (0, 0)))
    mlp_low = jnp.concatenate([up_low, down_low, bias_rows], axis=0)
    mlp_cols = jnp.concatenate(gather(mlp_low, "col"), axis=1)
    proj_full = (
        lax.all_gather(proj_low, ("row", "col"))
        .reshape(rows, cols * width, features)
        .transpose(1, 0, 2)
        .reshape(cols * width, width_all)
    )
    sent_rows = 2 * features
    up_bias_full = jnp.sum(mlp_cols[sent_rows : sent_rows + 3].astype(jnp.float32), axis=0)

    ones = jnp.int32(1)
    tables = jnp.arange(segments, dtype=jnp.int32)
    grand_ids = jnp.sum(
        jnp.where(parent_ids[:, None] == tables[None], parent_ids[None], 0), axis=1
    )
    anc_table = (
        jnp.left_shift(ones, tables)
        | jnp.left_shift(ones, parent_ids)
        | jnp.left_shift(ones, grand_ids)
    )
    all_places = jnp.arange(segment_ids.shape[0], dtype=jnp.int32)
    hot_all = jnp.left_shift(ones, segment_ids)
    anc_all = jnp.sum(
        jnp.where(segment_ids[None] == tables[:, None], anc_table[:, None], 0), axis=0
    )
    chunk_ids = [(c, e) for c in range(cols) for e in range(cores)]
    if whole_chunks:
        inner = [(c, e) for e in range(cores) for c in range(cols)]
    else:
        inner = chunk_ids
    order = [chunk_ids.index(chunk) for chunk in inner]
    order_rows = piece
    if not whole_chunks:
        order, order_rows = [0], queries

    def query_info(which):
        starts = [
            (e * cols + c) * tokens + which * half + row * piece for c, e in inner
        ]
        anc = [lax.dynamic_slice_in_dim(anc_all, s, piece, 0) for s in starts]
        pos = [s + jnp.arange(piece, dtype=jnp.int32) for s in starts]
        return anc, pos

    anc_own, pos_own = query_info(core)
    anc_other, pos_other = query_info(core ^ 1)
    anc = jnp.concatenate(anc_own + anc_other)
    pos = jnp.concatenate(pos_own + pos_other).astype(jnp.int32)
    limit = ((pos + 1) << segments) - 1
    codes = (all_places << segments) | hot_all
    core_places = pick(all_places.reshape(-1, cores, half), core, 1).reshape(-1)
    core_hot = pick(hot_all.reshape(-1, cores, half), core, 1).reshape(-1)
    core_codes = (core_places << segments) | core_hot
    lists_forward = block_lists(
        hot_all, all_places, anc[:queries], pos[:queries], KEY_BLOCK, block_rows
    )
    lists_backward = block_lists(
        core_hot, core_places, anc, pos, KEY_BLOCK_BACK, query_block(queries, 2 * queries)
    )
    setup = (lists_forward, lists_backward, anc[None], limit[None], codes[None], core_codes[None])

    layer_in, qkv_low, setup, mlp_cols = lax.optimization_barrier(
        (layer_in, qkv_low, setup, mlp_cols)
    )
    lists_forward, lists_backward, anc, limit, codes, core_codes = setup
    qkv_full = share(qkv_low, "row").reshape(width_all, 3 * width)
    normed_in, first_unit, first_spread = norm_forward(layer_in, vectors[0], vectors[1])
    normed_all = reorder(gather(normed_in, "col"), col).reshape(queries, width_all)
    cot_rows = spread(after(cotangent, normed_in, qkv_full), None, cores, rows)
    cot_low = low(cot_rows)
    normed_all, cot_low = lax.optimization_barrier((normed_all, cot_low))
    qkv = low(dot(normed_all, qkv_full) + bias_row)
    kv_own = jnp.stack([qkv[:, h * head_width : (h + 1) * head_width] for h in range(heads)])
    q_own = qkv[:, 2 * width :] * jnp.bfloat16(0.125)
    core_parts = gather(kv_own, "row")

    cot_both = jnp.concatenate(gather(cot_low, "dp"), axis=0)
    q_own, proj_full, cot_both, core_parts = lax.optimization_barrier(
        (q_own, proj_full, cot_both, core_parts)
    )
    parts = [part for held in core_parts for part in gather(held, "dp")]
    q_other = swap(q_own, "dp", 1)
    mlp_got = gather(after(mlp_cols[:sent_rows], *core_parts), "row")
    if whole_chunks:
        offsets = jnp.stack(
            [
                (e * cols + c) * tokens + (core ^ jd) * half + (row ^ k) * piece
                for k in range(rows)
                for jd in range(cores)
                for c, e in chunk_ids
            ]
        ).astype(jnp.int32)
        core_offsets = jnp.stack(
            [
                (e * cols + c) * half + (row ^ k) * piece
                for k in range(rows)
                for c, e in chunk_ids
            ]
        ).astype(jnp.int32)
        chunk, core_chunk = piece, piece
        grad_shape = (rows, heads, cols, cores, piece, head_width)
    else:

        def natural(pieces, count):
            sorted_parts = [
                [pieces[k * count + j] for j in range(count)] for k in range(rows)
            ]
            by_core = [reorder(p, core) if count > 1 else jnp.stack(p) for p in sorted_parts]
            stacked = reorder(by_core, row).reshape(
                rows, count, heads, cols, cores, piece, head_width
            )
            return [stacked.transpose(2, 4, 3, 1, 0, 5, 6).reshape(heads, -1, head_width)]

        parts, core_parts = natural(parts, cores), natural(core_parts, 1)
        offsets = core_offsets = jnp.zeros((1,), jnp.int32)
        chunk, core_chunk = parts[0].shape[1], core_parts[0].shape[1]
        grad_shape = core_parts[0].shape
    head_out, attended_low = attend_forward(
        *lists_forward,
        offsets,
        q_own,
        codes,
        anc[:, :queries],
        limit[:, :queries],
        parts,
        chunk,
        order,
        order_rows,
    )
    attended_low, mlp_got = lax.optimization_barrier((attended_low, mlp_got))
    attended = side_by_side(trade(attended_low.reshape(cols, own, width), "col"))
    out_other = swap(head_out, "dp", 1)

    hidden_all = cols * hidden_part

    def by_row(first, count):
        whole_rows = jnp.zeros((rows, count, hidden_all), jnp.bfloat16)
        for k in range(rows):
            part = mlp_got[k][None, first : first + count]
            whole_rows = lax.dynamic_update_slice_in_dim(whole_rows, part, row ^ k, 0)
        return whole_rows

    up_full = by_row(0, features).reshape(width_all, hidden_all)
    down_full = by_row(features, features).reshape(width_all, hidden_all)
    branch = dot(attended, proj_full) + vectors[4]
    middle = layer_in + branch
    normed_mid, second_unit, second_spread = norm_forward(middle, vectors[2], vectors[3])
    mid_both = jnp.concatenate(gather(normed_mid, "dp"), axis=0)
    hidden = dot(mid_both, up_full) + up_bias_full
    activated = low(gelu_tanh(hidden))
    act_grad = dot(cot_both, down_full)
    hidden_grad = low(jax.vjp(gelu_tanh, hidden)[1](act_grad)[0])

    def own_sum(both):
        return total(exchange([both[j * own : (j + 1) * own] for j in range(cores)], "dp"))

    mid_norm_grad = own_sum(dot(hidden_grad, up_full, 1, 1))
    second_back = norm_backward(mid_norm_grad, second_unit, second_spread, vectors[2])
    middle_grad = cot_rows + second_back
    mid_low = low(middle_grad)
    attended_grad = low(dot(mid_low, proj_full, 1, 1))

    sent = attended_grad.reshape(own, cols, width).transpose(1, 0, 2)
    sent, hidden_late, cot_late, activated_late = lax.optimization_barrier(
        (sent, hidden_grad, cot_both, activated)
    )
    out_grad = trade(sent, "col").reshape(queries, width)
    grad_other = swap(out_grad, "dp", 1)

    up_grad = low(dot(mid_both, hidden_late, 0, 0))
    down_grad = low(dot(cot_late, activated_late, 0, 0))
    proj_grad = low(dot(attended, mid_low, 0, 0)).reshape(cols, cores, head_part, width_all)
    proj_sum = total([pick(proj_grad, core, 1), swap(pick(proj_grad, core ^ 1, 1), "dp", 1)])
    pack = hidden_part // features
    proj_sent = (
        low(proj_sum)
        .reshape(cols, pack, head_part // pack, rows, features)
        .transpose(3, 2, 0, 1, 4)
    )
    proj_sent = jnp.stack([pick(proj_sent, col ^ k, 2) for k in range(cols)], axis=2)
    proj_sent = proj_sent.reshape(rows, head_part // pack, cols * pack * features)
    bias_grad = low(jnp.sum(hidden_late, axis=0, dtype=jnp.float32))
    bias_sent = jnp.pad(bias_grad[None], ((0, 15), (0, 0)))
    grads_sent = jnp.concatenate(
        [
            up_grad.reshape(rows, features, hidden_all),
            down_grad.reshape(rows, features, hidden_all),
            proj_sent,
            jnp.broadcast_to(bias_sent[None], (rows,) + bias_sent.shape),
        ],
        axis=1,
    )
    grads_sent = [pick(grads_sent, row ^ k) for k in range(rows)]
    grads_sent, grad_other = lax.optimization_barrier((grads_sent, grad_other))
    grads_got = exchange(grads_sent, "row")
    early = jnp.stack(
        [
            jnp.sum(mid_norm_grad * second_unit, axis=0),
            jnp.sum(mid_norm_grad, axis=0),
            jnp.sum(mid_low, axis=0, dtype=jnp.float32),
            jnp.sum(cot_low, axis=0, dtype=jnp.float32),
        ]
    )

    query_grad, query_grad_other, part_grads = attend_backward(
        *lists_backward,
        core_offsets,
        (q_own, q_other),
        (out_grad, grad_other),
        (head_out, out_other),
        core_codes,
        anc,
        limit,
        core_parts,
        core_chunk,
        order,
        order_rows,
        grad_shape,
    )
    if not whole_chunks:
        part_grads = part_grads.reshape(heads, cores, cols, rows, piece, head_width)
        part_grads = part_grads.transpose(3, 0, 2, 1, 4, 5)

    part_grads, grads_got, activated_late = lax.optimization_barrier(
        (part_grads, grads_got, activated_late)
    )
    kv_got = trade(part_grads.reshape(rows, heads, queries, head_width), "row")
    kv_grad = low(jnp.sum(kv_got.astype(jnp.float32), axis=0))
    query_low = low((query_grad + swap(query_grad_other, "dp", 1))[:, :width])
    qkv_grad = jnp.concatenate([kv_grad[h] for h in range(heads)] + [query_low], axis=1)
    first_parts = low(dot(qkv_grad, qkv_full, 1, 1)).reshape(cols, own, width_all)
    row_sums = low(total(grads_got))
    col_sums = low(
        total(
            exchange(
                [
                    row_sums[:, k * hidden_part : (k + 1) * hidden_part]
                    for k in range(cols)
                ],
                "col",
            )
        )
    )
    mlp_both = dot(activated_late, down_full, 1, 1)
    mlp_out = own_sum(mlp_both) + vectors[5]
    output_rows = by_device(low(branch + mlp_out), cores, rows)
    first_parts, col_sums, output_rows, qkv_grad, early = lax.optimization_barrier(
        (first_parts, col_sums, output_rows, qkv_grad, early)
    )
    first_grad = jnp.sum(trade(first_parts, "col").astype(jnp.float32), axis=0)

    other_sums = swap(col_sums, "dp", 1)
    first_sums = jnp.where(core == 0, col_sums, other_sums).astype(jnp.float32)
    second_sums = jnp.where(core == 0, other_sums, col_sums).astype(jnp.float32)
    both_sums = jnp.concatenate([first_sums, second_sums], axis=1)
    up_weight_grad = both_sums[:features]
    down_weight_grad = both_sums[features : 2 * features]
    up_bias_grad = both_sums[2 * features + head_part // pack]

    def proj_rows(sums):
        values = sums[2 * features : 2 * features + head_part // pack]
        values = values[:, : pack * features].reshape(head_part // pack, pack, features)
        return values.transpose(1, 0, 2).reshape(head_part, features)

    proj_weight_grad = (
        jnp.concatenate([proj_rows(first_sums), proj_rows(second_sums)], axis=0)
        .reshape(heads, HEAD_DIM, features)
        .transpose(0, 2, 1)
        .reshape(heads, features * HEAD_DIM)
    )
    def vector_sums(values):
        pieces = values.reshape(-1, rows, features).transpose(1, 0, 2)
        summed = total(exchange([pick(pieces, row ^ k) for k in range(rows)], "row"))
        return everywhere(everywhere(summed, "col"), "dp")

    first_back = norm_backward(first_grad, first_unit, first_spread, vectors[0])
    late = jnp.stack([jnp.sum(first_grad * first_unit, axis=0), jnp.sum(first_grad, axis=0)])
    output_grown, input_grown, late_sums = collect(
        output_rows, low(second_back + first_back), three_low(late), cores, rows
    )
    block_output = block_input + output_grown
    input_grad = cotangent + input_grown
    late_sums = everywhere(jnp.sum(late_sums, axis=0).reshape(2, features), "col")
    sums = vector_sums(early)
    wide = low(dot(normed_all, qkv_grad, 0, 0)).reshape(rows, features, 3 * width)
    bias_part = low(jnp.sum(qkv_grad, axis=0, dtype=jnp.float32))
    bias_part = jnp.broadcast_to(
        jnp.pad(bias_part[None], ((0, 15), (0, 0)))[None], (rows, 16, 3 * width)
    )
    wide = jnp.concatenate([wide, bias_part], axis=1)
    wide_pieces = [pick(wide, row ^ k) for k in range(rows)]
    wide_sum = low(total(exchange(wide_pieces, "row")))
    wide_sum = everywhere(wide_sum, "dp")

    def unpacked(values):
        lead = values.shape[0]
        kv = values[:, : 2 * width].reshape(lead, heads, 2, HEAD_DIM).transpose(2, 1, 0, 3)
        q = values[:, 2 * width :].reshape(lead, heads, HEAD_DIM).transpose(1, 0, 2)
        return jnp.concatenate([q[None], kv], axis=0)

    qkv_weight_grad = unpacked(wide_sum[:features]).reshape(3, heads, features * HEAD_DIM)
    qkv_bias_grad = unpacked(wide_sum[features : features + 1]).reshape(3, width)
    return (
        block_output,
        input_grad,
        late_sums[0],
        late_sums[1],
        qkv_weight_grad,
        qkv_bias_grad,
        proj_weight_grad,
        sums[2],
        sums[0],
        sums[1],
        up_weight_grad,
        up_bias_grad,
        down_weight_grad,
        sums[3],
    )


def solution(mesh):
    return jax.shard_map(
        shards,
        mesh=mesh,
        in_specs=(
            P("row", ("dp", "col")),
            P(),
            P(),
            P("row"),
            P("row"),
            P(None, "col", "row"),
            P(None, "col"),
            P("col", "row"),
            P("row"),
            P("row"),
            P("row"),
            P("row", "col"),
            P("col"),
            P("row", "col"),
            P("row"),
            P("row", ("dp", "col")),
        ),
        out_specs=(
            P("row", ("dp", "col")),
            P("row", ("dp", "col")),
            P("row"),
            P("row"),
            P(None, "col", "row"),
            P(None, "col"),
            P("col", "row"),
            P("row"),
            P("row"),
            P("row"),
            P("row", "col"),
            P("col"),
            P("row", "col"),
            P("row"),
        ),
        check_vma=False,
    )
```

profile of v0, /device:TPU:0, one launch (start us, length us, event | category | flops | bytes accessed | tf_op | source)
XLA Modules:
  0.0 566.3 jit_solution(18262998574957926547)
XLA Ops:
  18.7 4.1 all-to-all-start
  33.5 4.1 collective-permute-done.1
  44.1 3.6 all-to-all-start.1
  49.9 4.7 collective-permute-start.3
  58.1 3.3 all-to-all-done.1
  62.9 3.7 all-to-all-start.2
  67.0 7.5 %collective-permute-done.3 = bf16[320,768]{1,0:T(8,128)(2,1)} collective-permute-done((bf16[320,768]{1,0:T(8,128)(2,1)}, bf16[320,768]{1,0:T(8,128)(2,1)}, u32[]{:S(2)}, u32[]{:S(2)}) %collective-permute-start.3) | collective-permute-done | bytes 491552 | tf_op jit(solution)/shard_map/ppermute | solution.py:415
  74.5 17.9 %collective-permute-done.4 = bf16[320,768]{1,0:T(8,128)(2,1)} collective-permute-done((bf16[320,768]{1,0:T(8,128)(2,1)}, bf16[320,768]{1,0:T(8,128)(2,1)}, u32[]{:S(2)}, u32[]{:S(2)}) %collective-permute-start.4) | collective-permute-done | bytes 491552 | tf_op jit(solution)/shard_map/ppermute | solution.py:415
  100.7 3.3 fusion.7
  109.3 30.3 %all-gather.2.cloned.1.call-done = bf16[16,192,192]{2,1,0:T(8,128)(2,1)} async-done(((bf16[1,192,192]{2,1,0:T(8,128)(2,1)}), bf16[16,192,192]{2,1,0:T(8,128)(2,1)}) %all-gather.2.cloned.1.call-update) | async-done | bytes 1179664 | tf_op jit(solution)/shard_map/all_gather | solution.py:622
  146.6 7.3 %collective-permute-done.9.rest_6_.rest_3_ = bf16[3,1280,128]{2,1,0:T(8,128)(2,1)} collective-permute-done((bf16[3,1280,128]{2,1,0:T(8,128)(2,1)}, bf16[3,1280,128]{2,1,0:T(8,128)(2,1)}, u32[]{:S(2)}, u32[]{:S(2)}) %collective-permute-start.9) | collective-permute-done | bytes 983072 | tf_op jit(solution)/shard_map/ppermute | solution.py:415
  163.0 55.4 %shard_map.263 = (f32[1280,256]{1,0:T(8,128)}, bf16[1280,192]{1,0:T(8,128)(2,1)}) custom-call(s32[5,2]{1,0:T(8,128)} %copy.201.cnt, s32[5,20]{1,0:T(8,128)} %select_reduce_fusion.2.lst, s32[64]{0:T(128)} %stack.540.offs, bf16[1280,192]{1,0:T(8,128)(2,1)} %slice_multiply_fusion.q_ref.q_own, s32[1,10240]{1,0:T(1,128)} %bitcast.384, s32[1,1280]{1,0:T(1,128)} %slice.267.anc_ref, ...), custom_call_target="tpu_custom_call" | custom-call | flops 80530636800 | bytes 15728640 | tf_op jit(solution)/shard_map/pallas_call | solution.py:226
  220.6 12.2 %all-to-all-start.3 = ((bf16[4,320,192]{1,2,0:T(8,128)(2,1)}), bf16[4,320,192]{1,2,0:T(8,128)(2,1)S(1)}, u32[]{:S(2)}, u32[]{:S(2)}) async-start(bf16[4,320,192]{1,2,0:T(8,128)(2,1)} %copy.202), calls=%async_computation.3 | async-start | bytes 1179648 | tf_op jit(solution)/shard_map/all_to_all | solution.py:457
  242.6 3.8 all-to-all-done.3
  249.6 3.6 collective-permute-start.18
  255.5 3.4 fusion.63
  259.0 7.4 %multiply_convert_fusion = (bf16[640,1536]{1,0:T(8,128)(2,1)}, bf16[640,1536]{1,0:T(8,128)(2,1)S(1)}) fusion(f32[1536]{0:T(1024)S(1)} %copy-done.65, f32[640,1536]{1,0:T(8,128)S(1)} %fusion.63, bf16[768,1536]{1,0:T(8,128)(2,1)} %bitcast.177, bf16[320,768]{1,0:T(8,128)(2,1)S(1)} %collective-permute-done.18, bf16[320,768]{1,0:T(8,128)(2,1)S(1)} %add_convert_fusion.3), kind=kOutput, calls=%fused_computation.12 | convolution fusion | flops 1534525440 | bytes 11212800 | tf_op jit(solution)/shard_map/dot_general | solution.py:451
  266.4 4.1 fusion.64
  286.1 3.9 all-to-all-start.4
  290.1 5.1 convolution_convert_fusion.1
  295.2 3.5 convolution_convert_fusion.2
  322.4 83.4 %shard_map.264 = (f32[1280,256]{1,0:T(8,128)}, f32[1280,256]{1,0:T(8,128)}, bf16[4,3,4,2,160,128]{5,4,3,2,1,0:T(8,128)(2,1)}) custom-call(s32[10,2]{1,0:T(8,128)} %copy.210.cnt, s32[10,10]{1,0:T(8,128)} %select_reduce_fusion.1.lst, s32[32]{0:T(128)} %stack.465.offs, bf16[1280,192]{1,0:T(8,128)(2,1)} %slice_multiply_fusion.q_ref.q_own, ...), custom_call_target="tpu_custom_call" | custom-call | flops 100663296000 | bytes 7864320 | tf_op jit(solution)/shard_map/pallas_call | solution.py:369
  407.8 5.9 %all-to-all-start.5 = ((bf16[4,3,1280,128]{3,2,1,0:T(8,128)(2,1)}), bf16[4,3,1280,128]{3,2,1,0:T(8,128)(2,1)}, u32[]{:S(2)}, u32[]{:S(2)}) async-start(bf16[4,3,1280,128]{3,2,1,0:T(8,128)(2,1)} %bitcast.356), calls=%async_computation.5 | async-start | bytes 7864320 | tf_op jit(solution)/shard_map/all_to_all | solution.py:457
  414.1 4.1 fusion.65
  425.1 12.7 %collective-permute-done.27 = bf16[448,384]{1,0:T(8,128)(2,1)S(1)} collective-permute-done((bf16[448,384]{1,0:T(8,128)(2,1)S(1)}, bf16[448,384]{1,0:T(8,128)(2,1)S(1)}, u32[]{:S(2)}, u32[]{:S(2)}) %collective-permute-start.27) | collective-permute-done | bytes 344096 | tf_op jit(solution)/shard_map/ppermute | solution.py:415
  437.8 9.5 %collective-permute-done.28 = bf16[448,384]{1,0:T(8,128)(2,1)S(1)} collective-permute-done((bf16[448,384]{1,0:T(8,128)(2,1)S(1)}, bf16[448,384]{1,0:T(8,128)(2,1)S(1)}, u32[]{:S(2)}, u32[]{:S(2)}) %collective-permute-start.28) | collective-permute-done | bytes 344096 | tf_op jit(solution)/shard_map/ppermute | solution.py:415
  449.8 4.1 all-to-all-done.5
  461.2 5.4 all-to-all-start.6
  483.8 14.6 %collective-permute-done.42 = f32[4,192]{1,0:T(4,128)S(1)} collective-permute-done((f32[4,192]{1,0:T(4,128)S(1)}, f32[4,192]{1,0:T(4,128)S(1)}, u32[]{:S(2)}, u32[]{:S(2)}) %collective-permute-start.42) | collective-permute-done | bytes 3104 | tf_op jit(solution)/shard_map/ppermute | solution.py:415
  501.1 11.7 %collective-permute-done.43 = f32[4,192]{1,0:T(4,128)S(1)} collective-permute-done((f32[4,192]{1,0:T(4,128)S(1)}, f32[4,192]{1,0:T(4,128)S(1)}, u32[]{:S(2)}, u32[]{:S(2)}) %collective-permute-start.43) | collective-permute-done | bytes 3104 | tf_op jit(solution)/shard_map/ppermute | solution.py:415
  528.5 4.7 all-to-all-start.7
  535.3 13.2 %all-to-all-done.7 = bf16[8,176,384]{2,1,0:T(8,128)(2,1)S(1)} async-done(((bf16[8,176,384]{2,1,0:T(8,128)(2,1)}), bf16[8,176,384]{2,1,0:T(8,128)(2,1)S(1)}, u32[]{:S(2)}, u32[]{:S(2)}) %all-to-all-start.7) | async-done | bytes 1081376 | tf_op jit(solution)/shard_map/all_to_all | solution.py:457
  (488 shorter events, 188.6 us)
Async XLA Ops:
  10.0 23.5 %collective-permute-start = (bf16[400,384]{1,0:T(8,128)(2,1)}, bf16[400,384]{1,0:T(8,128)(2,1)}, u32[]{:S(2)}, u32[]{:S(2)}) collective-permute-start(bf16[400,384]{1,0:T(8,128)(2,1)} %pad_maximum_fusion.15), channel_id=1, source_target_pairs={{0,1},{1,0},{2,3},{3,2},{4,5},{5,4},{6,7},{7,6},{8,9},{9,8},{10,11... | collective-permute-start | bytes 921608 | tf_op jit(solution)/shard_map/ppermute | solution.py:415
  13.0 24.6 %collective-permute-start.1 = (bf16[400,384]{1,0:T(8,128)(2,1)}, bf16[400,384]{1,0:T(8,128)(2,1)}, u32[]{:S(2)}, u32[]{:S(2)}) collective-permute-start(bf16[400,384]{1,0:T(8,128)(2,1)} %pad_maximum_fusion.15), channel_id=1, source_target_pairs={{0,2},{1,3},{2,0},{3,1},{4,6},{5,7},{6,4},{7,5},{8,10},{9,11},{10,... | collective-permute-start | bytes 921608 | tf_op jit(solution)/shard_map/ppermute | solution.py:415
  15.6 22.0 %collective-permute-start.2 = (bf16[400,384]{1,0:T(8,128)(2,1)}, bf16[400,384]{1,0:T(8,128)(2,1)}, u32[]{:S(2)}, u32[]{:S(2)}) collective-permute-start(bf16[400,384]{1,0:T(8,128)(2,1)} %pad_maximum_fusion.15), channel_id=1, source_target_pairs={{0,3},{1,2},{2,1},{3,0},{4,7},{5,6},{6,5},{7,4},{8,11},{9,10},{10,... | collective-permute-start | bytes 921608 | tf_op jit(solution)/shard_map/ppermute | solution.py:415
  18.7 22.5 %all-to-all-start = ((f32[8,168,192]{2,1,0:T(8,128)}), f32[8,168,192]{2,1,0:T(8,128)S(1)}, u32[]{:S(2)}, u32[]{:S(2)}) async-start(f32[8,168,192]{2,1,0:T(8,128)} %pad_maximum_fusion.4), calls=%async_computation | async-start | bytes 2752512 | tf_op jit(solution)/shard_map/all_to_all | solution.py:457
  47.8 91.7 %all-gather.2.cloned.1.call-start = ((), (), s32[]{:S(2)}) async-start(), calls=%async_computation.8 | async-start | bytes 1671168 | tf_op jit(solution)/shard_map/all_gather | solution.py:622
  49.9 24.6 %collective-permute-start.3 = (bf16[320,768]{1,0:T(8,128)(2,1)}, bf16[320,768]{1,0:T(8,128)(2,1)}, u32[]{:S(2)}, u32[]{:S(2)}) collective-permute-start(bf16[320,768]{1,0:T(8,128)(2,1)} %add_convert_fusion.4), channel_id=1, source_target_pairs={{0,1},{1,0},{2,3},{3,2},{4,5},{5,4},{6,7},{7,6},{8,9},{9,8},{10,11... | collective-permute-start | bytes 1474568 | tf_op jit(solution)/shard_map/ppermute | solution.py:415
  54.6 37.9 %collective-permute-start.4 = (bf16[320,768]{1,0:T(8,128)(2,1)}, bf16[320,768]{1,0:T(8,128)(2,1)}, u32[]{:S(2)}, u32[]{:S(2)}) collective-permute-start(bf16[320,768]{1,0:T(8,128)(2,1)} %add_convert_fusion.4), channel_id=1, source_target_pairs={{0,2},{1,3},{2,0},{3,1},{4,6},{5,7},{6,4},{7,5},{8,10},{9,11},{10,... | collective-permute-start | bytes 1474568 | tf_op jit(solution)/shard_map/ppermute | solution.py:415
  55.6 36.9 %collective-permute-start.5 = (bf16[320,768]{1,0:T(8,128)(2,1)}, bf16[320,768]{1,0:T(8,128)(2,1)}, u32[]{:S(2)}, u32[]{:S(2)}) collective-permute-start(bf16[320,768]{1,0:T(8,128)(2,1)} %add_convert_fusion.4), channel_id=1, source_target_pairs={{0,3},{1,2},{2,1},{3,0},{4,7},{5,6},{6,5},{7,4},{8,11},{9,10},{10,... | collective-permute-start | bytes 1474568 | tf_op jit(solution)/shard_map/ppermute | solution.py:415
  62.9 32.8 %all-to-all-start.2 = ((f32[8,160,192]{2,1,0:T(8,128)}), f32[8,160,192]{2,1,0:T(8,128)S(1)}, u32[]{:S(2)}, u32[]{:S(2)}) async-start(f32[8,160,192]{2,1,0:T(8,128)} %bitcast.350), calls=%async_computation.2 | async-start | bytes 2621440 | tf_op jit(solution)/shard_map/all_to_all | solution.py:457
  105.6 41.0 %collective-permute-start.7 = (bf16[3,1280,128]{2,1,0:T(8,128)(2,1)}, bf16[3,1280,128]{2,1,0:T(8,128)(2,1)}, u32[]{:S(2)}, u32[]{:S(2)}) collective-permute-start(bf16[3,1280,128]{2,1,0:T(8,128)(2,1)} %pad_maximum_fusion.8.rest_0_), channel_id=1, source_target_pairs={{0,4},{4,0},{8,12},{12,8},{1,5},{5,1},{9,13},{13,9},{2,6},{6,2},{1... | collective-permute-start | bytes 2949128 | tf_op jit(solution)/shard_map/ppermute | solution.py:415
  107.8 38.8 %collective-permute-start.8 = (bf16[3,1280,128]{2,1,0:T(8,128)(2,1)}, bf16[3,1280,128]{2,1,0:T(8,128)(2,1)}, u32[]{:S(2)}, u32[]{:S(2)}) collective-permute-start(bf16[3,1280,128]{2,1,0:T(8,128)(2,1)} %pad_maximum_fusion.8.rest_0_), channel_id=1, source_target_pairs={{0,8},{4,12},{8,0},{12,4},{1,9},{5,13},{9,1},{13,5},{2,10},{6,14},... | collective-permute-start | bytes 2949128 | tf_op jit(solution)/shard_map/ppermute | solution.py:415
  109.2 44.6 %collective-permute-start.9 = (bf16[3,1280,128]{2,1,0:T(8,128)(2,1)}, bf16[3,1280,128]{2,1,0:T(8,128)(2,1)}, u32[]{:S(2)}, u32[]{:S(2)}) collective-permute-start(bf16[3,1280,128]{2,1,0:T(8,128)(2,1)} %pad_maximum_fusion.8.rest_0_), channel_id=1, source_target_pairs={{0,12},{4,8},{8,4},{12,0},{1,13},{5,9},{9,5},{13,1},{2,14},{6,10},... | collective-permute-start | bytes 2949128 | tf_op jit(solution)/shard_map/ppermute | solution.py:415
  159.5 58.9 %collective-permute-start.15 = (bf16[384,1536]{1,0:T(8,128)(2,1)}, bf16[384,1536]{1,0:T(8,128)(2,1)}, u32[]{:S(2)}, u32[]{:S(2)}) collective-permute-start(bf16[384,1536]{1,0:T(8,128)(2,1)} %slice.269), channel_id=1, source_target_pairs={{0,4},{4,0},{8,12},{12,8},{1,5},{5,1},{9,13},{13,9},{2,6},{6,2},{1... | collective-permute-start | bytes 3538952 | tf_op jit(solution)/shard_map/ppermute | solution.py:415
  161.0 57.4 %collective-permute-start.16 = (bf16[384,1536]{1,0:T(8,128)(2,1)}, bf16[384,1536]{1,0:T(8,128)(2,1)}, u32[]{:S(2)}, u32[]{:S(2)}) collective-permute-start(bf16[384,1536]{1,0:T(8,128)(2,1)} %slice.269), channel_id=1, source_target_pairs={{0,8},{4,12},{8,0},{12,4},{1,9},{5,13},{9,1},{13,5},{2,10},{6,14},... | collective-permute-start | bytes 3538952 | tf_op jit(solution)/shard_map/ppermute | solution.py:415
  161.5 56.9 %collective-permute-start.17 = (bf16[384,1536]{1,0:T(8,128)(2,1)}, bf16[384,1536]{1,0:T(8,128)(2,1)}, u32[]{:S(2)}, u32[]{:S(2)}) collective-permute-start(bf16[384,1536]{1,0:T(8,128)(2,1)} %slice.269), channel_id=1, source_target_pairs={{0,12},{4,8},{8,4},{12,0},{1,13},{5,9},{9,5},{13,1},{2,14},{6,10},... | collective-permute-start | bytes 3538952 | tf_op jit(solution)/shard_map/ppermute | solution.py:415
  220.6 25.8 %all-to-all-start.3 = ((bf16[4,320,192]{1,2,0:T(8,128)(2,1)}), bf16[4,320,192]{1,2,0:T(8,128)(2,1)S(1)}, u32[]{:S(2)}, u32[]{:S(2)}) async-start(bf16[4,320,192]{1,2,0:T(8,128)(2,1)} %copy.202), calls=%async_computation.3 | async-start | bytes 1179648 | tf_op jit(solution)/shard_map/all_to_all | solution.py:457
  276.8 45.6 %collective-permute-start.22 = (f32[1280,256]{1,0:T(8,128)}, f32[1280,256]{1,0:T(8,128)}, u32[]{:S(2)}, u32[]{:S(2)}) collective-permute-start(f32[1280,256]{1,0:T(8,128)} %get-tuple-element.98.o_own), channel_id=1, source_target_pairs={{0,16},{16,0},{1,17},{17,1},{2,18},{18,2},{3,19},{19,3},{4,20},{20... | collective-permute-start | bytes 3932168 | tf_op jit(solution)/shard_map/ppermute | solution.py:415
  286.1 20.6 %all-to-all-start.4 = ((bf16[4,320,192]{1,2,0:T(8,128)(2,1)}), bf16[4,320,192]{1,2,0:T(8,128)(2,1)S(1)}, u32[]{:S(2)}, u32[]{:S(2)}) async-start(bf16[4,320,192]{1,2,0:T(8,128)(2,1)} %bitcast.179), calls=%async_computation.4 | async-start | bytes 1179648 | tf_op jit(solution)/shard_map/all_to_all | solution.py:457
  315.4 90.4 %collective-permute-start.23 = (bf16[448,1536]{1,0:T(8,128)(2,1)}, bf16[448,1536]{1,0:T(8,128)(2,1)S(1)}, u32[]{:S(2)}, u32[]{:S(2)}) collective-permute-start(bf16[448,1536]{1,0:T(8,128)(2,1)} %get-tuple-element.102), channel_id=1, source_target_pairs={{0,4},{4,0},{8,12},{12,8},{1,5},{5,1},{9,13},{13,9},{2,6},{6,2},{1... | collective-permute-start | bytes 4128776 | tf_op jit(solution)/shard_map/ppermute | solution.py:415
  318.5 87.3 %collective-permute-start.24 = (bf16[448,1536]{1,0:T(8,128)(2,1)}, bf16[448,1536]{1,0:T(8,128)(2,1)S(1)}, u32[]{:S(2)}, u32[]{:S(2)}) collective-permute-start(bf16[448,1536]{1,0:T(8,128)(2,1)} %get-tuple-element.103), channel_id=1, source_target_pairs={{0,8},{4,12},{8,0},{12,4},{1,9},{5,13},{9,1},{13,5},{2,10},{6,14},... | collective-permute-start | bytes 4128776 | tf_op jit(solution)/shard_map/ppermute | solution.py:415
  320.9 85.0 %collective-permute-start.25 = (bf16[448,1536]{1,0:T(8,128)(2,1)S(1)}, bf16[448,1536]{1,0:T(8,128)(2,1)S(1)}, u32[]{:S(2)}, u32[]{:S(2)}) collective-permute-start(bf16[448,1536]{1,0:T(8,128)(2,1)S(1)} %get-tuple-element.104), channel_id=1, source_target_pairs={{0,12},{4,8},{8,4},{12,0},{1,13},{5,9},{9,5},{13,1},{2,14},{6,10},... | collective-permute-start | bytes 4128776 | tf_op jit(solution)/shard_map/ppermute | solution.py:415
  407.8 46.2 %all-to-all-start.5 = ((bf16[4,3,1280,128]{3,2,1,0:T(8,128)(2,1)}), bf16[4,3,1280,128]{3,2,1,0:T(8,128)(2,1)}, u32[]{:S(2)}, u32[]{:S(2)}) async-start(bf16[4,3,1280,128]{3,2,1,0:T(8,128)(2,1)} %bitcast.356), calls=%async_computation.5 | async-start | bytes 7864320 | tf_op jit(solution)/shard_map/all_to_all | solution.py:457
  418.3 29.8 %collective-permute-start.30 = (f32[320,768]{1,0:T(8,128)S(1)}, f32[320,768]{1,0:T(8,128)S(1)}, u32[]{:S(2)}, u32[]{:S(2)}) collective-permute-start(f32[320,768]{1,0:T(8,128)S(1)} %slice.353), channel_id=1, source_target_pairs={{0,16},{16,0},{1,17},{17,1},{2,18},{18,2},{3,19},{19,3},{4,20},{20... | collective-permute-start | bytes 2949128 | tf_op jit(solution)/shard_map/ppermute | solution.py:415
  420.7 26.6 %collective-permute-start.28 = (bf16[448,384]{1,0:T(8,128)(2,1)S(1)}, bf16[448,384]{1,0:T(8,128)(2,1)S(1)}, u32[]{:S(2)}, u32[]{:S(2)}) collective-permute-start(bf16[448,384]{1,0:T(8,128)(2,1)S(1)} %get-tuple-element.247), channel_id=1, source_target_pairs={{0,2},{1,3},{2,0},{3,1},{4,6},{5,7},{6,4},{7,5},{8,10},{9,11},{10,... | collective-permute-start | bytes 1032200 | tf_op jit(solution)/shard_map/ppermute | solution.py:415
  423.0 24.2 %collective-permute-start.29 = (bf16[448,384]{1,0:T(8,128)(2,1)S(1)}, bf16[448,384]{1,0:T(8,128)(2,1)S(1)}, u32[]{:S(2)}, u32[]{:S(2)}) collective-permute-start(bf16[448,384]{1,0:T(8,128)(2,1)S(1)} %get-tuple-element.246), channel_id=1, source_target_pairs={{0,3},{1,2},{2,1},{3,0},{4,7},{5,6},{6,5},{7,4},{8,11},{9,10},{10,... | collective-permute-start | bytes 1032200 | tf_op jit(solution)/shard_map/ppermute | solution.py:415
  461.2 61.1 %all-to-all-start.6 = ((bf16[4,320,768]{2,1,0:T(8,128)(2,1)}), bf16[4,320,768]{2,1,0:T(8,128)(2,1)}, u32[]{:S(2)}, u32[]{:S(2)}) async-start(bf16[4,320,768]{2,1,0:T(8,128)(2,1)} %bitcast.365), calls=%async_computation.6 | async-start | bytes 3932160 | tf_op jit(solution)/shard_map/all_to_all | solution.py:457
  475.8 22.5 %collective-permute-start.42 = (f32[4,192]{1,0:T(4,128)S(1)}, f32[4,192]{1,0:T(4,128)S(1)}, u32[]{:S(2)}, u32[]{:S(2)}) collective-permute-start(f32[4,192]{1,0:T(4,128)S(1)} %fusion.40), channel_id=1, source_target_pairs={{0,1},{1,0},{2,3},{3,2},{4,5},{5,4},{6,7},{7,6},{8,9},{9,8},{10,11... | collective-permute-start | bytes 9224 | tf_op jit(solution)/shard_map/ppermute | solution.py:415
  478.3 34.5 %collective-permute-start.43 = (f32[4,192]{1,0:T(4,128)S(1)}, f32[4,192]{1,0:T(4,128)S(1)}, u32[]{:S(2)}, u32[]{:S(2)}) collective-permute-start(f32[4,192]{1,0:T(4,128)S(1)} %fusion.40), channel_id=1, source_target_pairs={{0,2},{1,3},{2,0},{3,1},{4,6},{5,7},{6,4},{7,5},{8,10},{9,11},{10,... | collective-permute-start | bytes 9224 | tf_op jit(solution)/shard_map/ppermute | solution.py:415
  480.3 32.5 %collective-permute-start.44 = (f32[4,192]{1,0:T(4,128)S(1)}, f32[4,192]{1,0:T(4,128)S(1)}, u32[]{:S(2)}, u32[]{:S(2)}) collective-permute-start(f32[4,192]{1,0:T(4,128)S(1)} %fusion.40), channel_id=1, source_target_pairs={{0,3},{1,2},{2,1},{3,0},{4,7},{5,6},{6,5},{7,4},{8,11},{9,10},{10,... | collective-permute-start | bytes 9224 | tf_op jit(solution)/shard_map/ppermute | solution.py:415
  481.6 33.9 %collective-permute-start.34 = (bf16[208,576]{1,0:T(8,128)(2,1)}, bf16[208,576]{1,0:T(8,128)(2,1)S(1)}, u32[]{:S(2)}, u32[]{:S(2)}) collective-permute-start(bf16[208,576]{1,0:T(8,128)(2,1)} %get-tuple-element.254), channel_id=1, source_target_pairs={{0,4},{4,0},{8,12},{12,8},{1,5},{5,1},{9,13},{13,9},{2,6},{6,2},{1... | collective-permute-start | bytes 718856 | tf_op jit(solution)/shard_map/ppermute | solution.py:415
  482.7 32.8 %collective-permute-start.35 = (bf16[208,576]{1,0:T(8,128)(2,1)}, bf16[208,576]{1,0:T(8,128)(2,1)S(1)}, u32[]{:S(2)}, u32[]{:S(2)}) collective-permute-start(bf16[208,576]{1,0:T(8,128)(2,1)} %get-tuple-element.255), channel_id=1, source_target_pairs={{0,8},{4,12},{8,0},{12,4},{1,9},{5,13},{9,1},{13,5},{2,10},{6,14},... | collective-permute-start | bytes 718856 | tf_op jit(solution)/shard_map/ppermute | solution.py:415
  528.5 20.0 %all-to-all-start.7 = ((bf16[8,176,384]{2,1,0:T(8,128)(2,1)}), bf16[8,176,384]{2,1,0:T(8,128)(2,1)S(1)}, u32[]{:S(2)}, u32[]{:S(2)}) async-start(bf16[8,176,384]{2,1,0:T(8,128)(2,1)} %pad_maximum_fusion.6), calls=%async_computation.7 | async-start | bytes 2162688 | tf_op jit(solution)/shard_map/all_to_all | solution.py:457
  (102 other events, 1096.7 us)
Sparse Core Ops, SparseCore 0:
  58.1 81.3 all-gather.1
where the time goes:
time: 574 us; the launch traced here: 566 us
  waiting for transfers between devices  145 us (25%)
  Pallas kernels  139 us (24%)
  starting transfers between devices  101 us (18%)
  local copies, waits for them, and re-layouts  73.7 us (13%)
  other arithmetic  49.7 us (9%)
  matrix products  42.1 us (7%)
  between operations  16.1 us (3%)
    ppermute x46, waiting for transfers between devices, swap(): lax.ppermute(value, axis, [(source, source ^ step) for source in range(co...  86.5 us
    pallas_call x1, Pallas kernels, attend_backward(): pl.pallas_call(functools.partial(backward_kernel, heads, part_count, rows...  83.4 us
    ppermute x46, starting transfers between devices, swap(): lax.ppermute(value, axis, [(source, source ^ step) for source in range(co...  57.6 us
    pallas_call x1, Pallas kernels, attend_forward(): pl.pallas_call(functools.partial(forward_kernel, heads, part_count, rows,...  55.4 us
    all_to_all x8, starting transfers between devices, trade(): return lax.all_to_all(values, axis, 0, 0)  43.7 us
    dot_general x12, matrix products, dot(): lax.dot_general(left, right, (((left_dim,), (right_dim,)), ((), ())), pre...  42.1 us
    all_gather x1, waiting for transfers between devices, shards(): lax.all_gather(proj_low, ('row', 'col'))  30.3 us
    all_to_all x8, waiting for transfers between devices, trade(): return lax.all_to_all(values, axis, 0, 0)  27.8 us
  transfers between devices with their start and end apart: 55, of which 17 were waited for; matrix products, arithmetic and copies ran while one was open for 22% of the time, Pallas kernels for 25%

commit v1 on v0

--- a/solution.py
+++ b/solution.py
@@ -103,15 +103,16 @@
     lax.fori_loop(full, some, masked, 0)
 
 
-def shuffle(source, target, order, rows, first=0):
+def shuffle(source, target, order, rows, first=0, stride=2):
     for place, origin in enumerate(order):
-        at = first + place * rows
+        at = (place * stride + first) * rows
         target[at : at + rows, :] = source[origin * rows : (origin + 1) * rows, :]
 
 
-def unshuffle(source, target, order, rows, first=0):
+def unshuffle(source, target, order, rows, first=0, stride=2):
     for place, origin in enumerate(order):
-        part = source[first + place * rows : first + (place + 1) * rows, :]
+        at = (place * stride + first) * rows
+        part = source[at : at + rows, :]
         part = part[:, : target.shape[1]].astype(target.dtype)
         target[origin * rows : (origin + 1) * rows, :] = part
 
@@ -141,7 +142,7 @@
     def _():
         start_parts(offs, parts, held, sem, rows)
         right[...] = jnp.zeros_like(right)
-        shuffle(q_ref, qs, order, order_rows)
+        shuffle(q_ref, qs, order, order_rows, 0, 1)
         fill_keys(code, keys)
         wait_parts(parts, held, sem)
 
@@ -188,8 +189,8 @@
 
     @pl.when(b == pl.num_programs(0) - 1)
     def _():
-        unshuffle(os, o_ref, order, order_rows)
-        unshuffle(os, low_ref, order, order_rows)
+        unshuffle(os, o_ref, order, order_rows, 0, 1)
+        unshuffle(os, low_ref, order, order_rows, 0, 1)
 
 
 def query_block(count, whole_count=None):
@@ -284,11 +285,11 @@
         right[...] = jnp.zeros_like(right)
         acc[...] = jnp.zeros_like(acc)
         shuffle(q_own, qs, order, order_rows)
-        shuffle(q_other, qs, order, order_rows, q_own.shape[0])
+        shuffle(q_other, qs, order, order_rows, 1)
         shuffle(g_own, gs, order, order_rows)
-        shuffle(g_other, gs, order, order_rows, q_own.shape[0])
+        shuffle(g_other, gs, order, order_rows, 1)
         shuffle(o_own, os, order, order_rows)
-        shuffle(o_other, os, order, order_rows, q_own.shape[0])
+        shuffle(o_other, os, order, order_rows, 1)
         fill_keys(code, keys)
         wait_parts(parts, held, sem)
 
@@ -353,7 +354,7 @@
     def _():
         store_grads(acc, held, grads, out_sem)
         unshuffle(dsum, dq_own, order, order_rows)
-        unshuffle(dsum, dq_other, order, order_rows, q_own.shape[0])
+        unshuffle(dsum, dq_other, order, order_rows, 1)
 
 
 def attend_backward(
@@ -662,25 +663,34 @@
 
     anc_own, pos_own = query_info(core)
     anc_other, pos_other = query_info(core ^ 1)
-    anc = jnp.concatenate(anc_own + anc_other)
-    pos = jnp.concatenate(pos_own + pos_other).astype(jnp.int32)
+    if whole_chunks:
+        anc_both = [chunk for pair in zip(anc_own, anc_other) for chunk in pair]
+        pos_both = [chunk for pair in zip(pos_own, pos_other) for chunk in pair]
+    else:
+        anc_both, pos_both = anc_own + anc_other, pos_own + pos_other
+    anc, anc_both = jnp.concatenate(anc_own), jnp.concatenate(anc_both)
+    pos = jnp.concatenate(pos_own).astype(jnp.int32)
+    pos_both = jnp.concatenate(pos_both).astype(jnp.int32)
     limit = ((pos + 1) << segments) - 1
+    limit_both = ((pos_both + 1) << segments) - 1
     codes = (all_places << segments) | hot_all
     core_places = pick(all_places.reshape(-1, cores, half), core, 1).reshape(-1)
     core_hot = pick(hot_all.reshape(-1, cores, half), core, 1).reshape(-1)
     core_codes = (core_places << segments) | core_hot
     lists_forward = block_lists(
-        hot_all, all_places, anc[:queries], pos[:queries], KEY_BLOCK, block_rows
+        hot_all, all_places, anc, pos, KEY_BLOCK, block_rows
     )
     lists_backward = block_lists(
-        core_hot, core_places, anc, pos, KEY_BLOCK_BACK, query_block(queries, 2 * queries)
-    )
-    setup = (lists_forward, lists_backward, anc[None], limit[None], codes[None], core_codes[None])
+        core_hot, core_places, anc_both, pos_both, KEY_BLOCK_BACK, query_block(queries, 2 * queries)
+    )
+    rows_forward = (anc[None], limit[None])
+    rows_backward = (anc_both[None], limit_both[None])
+    setup = (lists_forward, lists_backward, rows_forward, rows_backward, codes[None], core_codes[None])
 
     layer_in, qkv_low, setup, mlp_cols = lax.optimization_barrier(
         (layer_in, qkv_low, setup, mlp_cols)
     )
-    lists_forward, lists_backward, anc, limit, codes, core_codes = setup
+    lists_forward, lists_backward, rows_forward, rows_backward, codes, core_codes = setup
     qkv_full = share(qkv_low, "row").reshape(width_all, 3 * width)
     normed_in, first_unit, first_spread = norm_forward(layer_in, vectors[0], vectors[1])
     normed_all = reorder(gather(normed_in, "col"), col).reshape(queries, width_all)
@@ -738,8 +748,7 @@
         offsets,
         q_own,
         codes,
-        anc[:, :queries],
-        limit[:, :queries],
+        *rows_forward,
         parts,
         chunk,
         order,
@@ -799,17 +808,15 @@
     proj_sent = proj_sent.reshape(rows, head_part // pack, cols * pack * features)
     bias_grad = low(jnp.sum(hidden_late, axis=0, dtype=jnp.float32))
     bias_sent = jnp.pad(bias_grad[None], ((0, 15), (0, 0)))
-    grads_sent = jnp.concatenate(
-        [
-            up_grad.reshape(rows, features, hidden_all),
-            down_grad.reshape(rows, features, hidden_all),
-            proj_sent,
-            jnp.broadcast_to(bias_sent[None], (rows,) + bias_sent.shape),
-        ],
-        axis=1,
-    )
-    grads_sent = [pick(grads_sent, row ^ k) for k in range(rows)]
-    grads_sent, grad_other = lax.optimization_barrier((grads_sent, grad_other))
+    up_grad = up_grad.reshape(rows, features, hidden_all)
+    down_grad = down_grad.reshape(rows, features, hidden_all)
+    grads_sent = [
+        jnp.concatenate(
+            [pick(part, row ^ k) for part in (up_grad, down_grad, proj_sent)] + [bias_sent], axis=0
+        )
+        for k in range(rows)
+    ]
+    grads_sent, rows_backward = lax.optimization_barrier((grads_sent, rows_backward))
     grads_got = exchange(grads_sent, "row")
     early = jnp.stack(
         [
@@ -827,8 +834,7 @@
         (out_grad, grad_other),
         (head_out, out_other),
         core_codes,
-        anc,
-        limit,
+        *rows_backward,
         core_parts,
         core_chunk,
         order,

time: 574 us -> 567 us (0.988)
  Pallas kernels: 139 us -> 130 us
  waiting for transfers between devices: 145 us -> 151 us
    all_to_all x8, waiting for transfers between devices: 27.8 us -> 38.5 us  [trade(): return lax.all_to_all(values, axis, 0, 0)]
    pallas_call x1, Pallas kernels: 83.4 us -> 73.5 us  [attend_backward(): pl.pallas_call(functools.partial(backward_kernel, heads, part_count, rows...]
    ppermute x46, starting transfers between devices: 57.6 us -> 51 us  [swap(): lax.ppermute(value, axis, [(source, source ^ step) for source in range(co...]
    unnamed x171 -> x151, local copies, waits for them, and re-layouts: 15 us -> 13.9 us
  transfers between devices with their start and end apart: 55 -> 55, of which waited for: 17 -> 17; matrix products, arithmetic and copies ran while one was open for 22% -> 22% of each run, Pallas kernels for 25% -> 23%
where the time goes in v1:
time: 567 us; the launch traced here: 557 us
  waiting for transfers between devices  151 us (27%)
  Pallas kernels  130 us (23%)
  starting transfers between devices  95.4 us (17%)
  local copies, waits for them, and re-layouts  74.3 us (13%)
  other arithmetic  51.4 us (9%)
  matrix products  38.8 us (7%)
  between operations  16 us (3%)
    ppermute x46, waiting for transfers between devices, swap(): lax.ppermute(value, axis, [(source, source ^ step) for source in range(co...  82.1 us
    pallas_call x1, Pallas kernels, attend_backward(): pl.pallas_call(functools.partial(backward_kernel, heads, part_count, rows...  73.5 us
    pallas_call x1, Pallas kernels, attend_forward(): pl.pallas_call(functools.partial(forward_kernel, heads, part_count, rows,...  56.8 us
    ppermute x46, starting transfers between devices, swap(): lax.ppermute(value, axis, [(source, source ^ step) for source in range(co...  51 us
    all_to_all x8, starting transfers between devices, trade(): return lax.all_to_all(values, axis, 0, 0)  44.4 us
    dot_general x12, matrix products, dot(): lax.dot_general(left, right, (((left_dim,), (right_dim,)), ((), ())), pre...  38.8 us
    all_to_all x8, waiting for transfers between devices, trade(): return lax.all_to_all(values, axis, 0, 0)  38.5 us
    all_gather x1, waiting for transfers between devices, shards(): lax.all_gather(proj_low, ('row', 'col'))  30.3 us
  transfers between devices with their start and end apart: 55, of which 17 were waited for; matrix products, arithmetic and copies ran while one was open for 22% of the time, Pallas kernels for 23%

profile of v1, /device:TPU:0, one launch (start us, length us, event | category | flops | bytes accessed | tf_op | source)
XLA Modules:
  0.0 557.1 jit_solution(7488496035821876743)
XLA Ops:
  10.0 3.0 collective-permute-start
  18.7 4.1 all-to-all-start
  44.1 3.6 all-to-all-start.1
  49.9 4.6 collective-permute-start.3
  58.0 3.4 all-to-all-done.1
  62.9 3.7 all-to-all-start.2
  67.0 7.3 %collective-permute-done.3 = bf16[320,768]{1,0:T(8,128)(2,1)} collective-permute-done((bf16[320,768]{1,0:T(8,128)(2,1)}, bf16[320,768]{1,0:T(8,128)(2,1)}, u32[]{:S(2)}, u32[]{:S(2)}) %collective-permute-start.3) | collective-permute-done | bytes 491552 | tf_op jit(solution)/shard_map/ppermute | solution.py:416
  74.4 18.0 %collective-permute-done.4 = bf16[320,768]{1,0:T(8,128)(2,1)} collective-permute-done((bf16[320,768]{1,0:T(8,128)(2,1)}, bf16[320,768]{1,0:T(8,128)(2,1)}, u32[]{:S(2)}, u32[]{:S(2)}) %collective-permute-start.4) | collective-permute-done | bytes 491552 | tf_op jit(solution)/shard_map/ppermute | solution.py:416
  100.7 3.3 fusion.7
  109.2 30.3 %all-gather.2.cloned.1.call-done = bf16[16,192,192]{2,1,0:T(8,128)(2,1)} async-done(((bf16[1,192,192]{2,1,0:T(8,128)(2,1)}), bf16[16,192,192]{2,1,0:T(8,128)(2,1)}) %all-gather.2.cloned.1.call-update) | async-done | bytes 1179664 | tf_op jit(solution)/shard_map/all_gather | solution.py:623
  146.5 7.2 %collective-permute-done.9.rest_6_.rest_3_ = bf16[3,1280,128]{2,1,0:T(8,128)(2,1)} collective-permute-done((bf16[3,1280,128]{2,1,0:T(8,128)(2,1)}, bf16[3,1280,128]{2,1,0:T(8,128)(2,1)}, u32[]{:S(2)}, u32[]{:S(2)}) %collective-permute-start.9) | collective-permute-done | bytes 983072 | tf_op jit(solution)/shard_map/ppermute | solution.py:416
  161.7 56.8 %shard_map.263 = (f32[1280,256]{1,0:T(8,128)}, bf16[1280,192]{1,0:T(8,128)(2,1)}) custom-call(s32[5,2]{1,0:T(8,128)} %copy.186.cnt, s32[5,20]{1,0:T(8,128)} %select_reduce_fusion.2.lst, s32[64]{0:T(128)} %stack.540.offs, bf16[1280,192]{1,0:T(8,128)(2,1)} %slice_multiply_fusion.q_ref.q_own, s32[1,10240]{1,0:T(1,128)} %bitcast.392, ...), custom_call_target="tpu_custom_call" | custom-call | flops 80530636800 | bytes 15728640 | tf_op jit(solution)/shard_map/pallas_call | solution.py:227
  220.7 12.2 %all-to-all-start.3 = ((bf16[4,320,192]{1,2,0:T(8,128)(2,1)}), bf16[4,320,192]{1,2,0:T(8,128)(2,1)S(1)}, u32[]{:S(2)}, u32[]{:S(2)}) async-start(bf16[4,320,192]{1,2,0:T(8,128)(2,1)} %copy.187), calls=%async_computation.3 | async-start | bytes 1179648 | tf_op jit(solution)/shard_map/all_to_all | solution.py:458
  242.6 6.5 %all-to-all-done.3 = bf16[4,320,192]{1,2,0:T(8,128)(2,1)S(1)} async-done(((bf16[4,320,192]{1,2,0:T(8,128)(2,1)}), bf16[4,320,192]{1,2,0:T(8,128)(2,1)S(1)}, u32[]{:S(2)}, u32[]{:S(2)}) %all-to-all-start.3) | async-done | bytes 491552 | tf_op jit(solution)/shard_map/all_to_all | solution.py:458
  255.7 3.4 fusion.69
  259.1 7.5 %multiply_convert_fusion = (bf16[640,1536]{1,0:T(8,128)(2,1)}, bf16[640,1536]{1,0:T(8,128)(2,1)S(1)}) fusion(f32[1536]{0:T(1024)S(1)} %copy-done.56, f32[640,1536]{1,0:T(8,128)S(1)} %fusion.69, bf16[768,1536]{1,0:T(8,128)(2,1)} %bitcast.177, bf16[320,768]{1,0:T(8,128)(2,1)S(1)} %collective-permute-done.18, bf16[320,768]{1,0:T(8,128)(2,1)S(1)} %add_convert_fusion.3), kind=kOutput, calls=%fused_computation.11 | convolution fusion | flops 1534525440 | bytes 11212800 | tf_op jit(solution)/shard_map/dot_general | solution.py:452
  266.6 4.1 fusion.70
  286.7 3.9 all-to-all-start.4
  290.7 3.9 convolution_convert_fusion.1
  308.6 3.6 fusion.12
  319.5 73.5 %shard_map.264 = (f32[1280,256]{1,0:T(8,128)}, f32[1280,256]{1,0:T(8,128)}, bf16[4,3,4,2,160,128]{5,4,3,2,1,0:T(8,128)(2,1)}) custom-call(s32[10,2]{1,0:T(8,128)} %copy.192.cnt, s32[10,10]{1,0:T(8,128)} %select_reduce_fusion.1.lst, s32[32]{0:T(128)} %stack.465.offs, bf16[1280,192]{1,0:T(8,128)(2,1)} %slice_multiply_fusion.q_ref.q_own, ...), custom_call_target="tpu_custom_call" | custom-call | flops 100663296000 | bytes 7864320 | tf_op jit(solution)/shard_map/pallas_call | solution.py:370
  393.1 7.8 %all-to-all-start.5 = ((bf16[4,3,1280,128]{3,2,1,0:T(8,128)(2,1)}), bf16[4,3,1280,128]{3,2,1,0:T(8,128)(2,1)}, u32[]{:S(2)}, u32[]{:S(2)}) async-start(bf16[4,3,1280,128]{3,2,1,0:T(8,128)(2,1)} %bitcast.368), calls=%async_computation.5 | async-start | bytes 7864320 | tf_op jit(solution)/shard_map/all_to_all | solution.py:458
  408.3 3.4 fusion.71
  413.0 7.8 %collective-permute-done.27 = bf16[448,384]{1,0:T(8,128)(2,1)S(1)} collective-permute-done((bf16[448,384]{1,0:T(8,128)(2,1)S(1)}, bf16[448,384]{1,0:T(8,128)(2,1)S(1)}, u32[]{:S(2)}, u32[]{:S(2)}) %collective-permute-start.27) | collective-permute-done | bytes 344096 | tf_op jit(solution)/shard_map/ppermute | solution.py:416
  420.7 9.9 %collective-permute-done.28 = bf16[448,384]{1,0:T(8,128)(2,1)S(1)} collective-permute-done((bf16[448,384]{1,0:T(8,128)(2,1)S(1)}, bf16[448,384]{1,0:T(8,128)(2,1)S(1)}, u32[]{:S(2)}, u32[]{:S(2)}) %collective-permute-start.28) | collective-permute-done | bytes 344096 | tf_op jit(solution)/shard_map/ppermute | solution.py:416
  434.5 11.8 %all-to-all-done.5 = bf16[4,3,1280,128]{3,2,1,0:T(8,128)(2,1)} async-done(((bf16[4,3,1280,128]{3,2,1,0:T(8,128)(2,1)}), bf16[4,3,1280,128]{3,2,1,0:T(8,128)(2,1)}, u32[]{:S(2)}, u32[]{:S(2)}) %all-to-all-start.5) | async-done | bytes 3932192 | tf_op jit(solution)/shard_map/all_to_all | solution.py:458
  450.5 3.0 convolution_convert_fusion
  453.6 4.6 all-to-all-start.6
  473.9 16.3 %collective-permute-done.42 = f32[4,192]{1,0:T(4,128)S(1)} collective-permute-done((f32[4,192]{1,0:T(4,128)S(1)}, f32[4,192]{1,0:T(4,128)S(1)}, u32[]{:S(2)}, u32[]{:S(2)}) %collective-permute-start.42) | collective-permute-done | bytes 3104 | tf_op jit(solution)/shard_map/ppermute | solution.py:416
  492.4 11.5 %collective-permute-done.43 = f32[4,192]{1,0:T(4,128)S(1)} collective-permute-done((f32[4,192]{1,0:T(4,128)S(1)}, f32[4,192]{1,0:T(4,128)S(1)}, u32[]{:S(2)}, u32[]{:S(2)}) %collective-permute-start.43) | collective-permute-done | bytes 3104 | tf_op jit(solution)/shard_map/ppermute | solution.py:416
  519.6 4.5 all-to-all-start.7
  526.1 13.2 %all-to-all-done.7 = bf16[8,176,384]{2,1,0:T(8,128)(2,1)S(1)} async-done(((bf16[8,176,384]{2,1,0:T(8,128)(2,1)}), bf16[8,176,384]{2,1,0:T(8,128)(2,1)S(1)}, u32[]{:S(2)}, u32[]{:S(2)}) %all-to-all-start.7) | async-done | bytes 1081376 | tf_op jit(solution)/shard_map/all_to_all | solution.py:458
  (470 shorter events, 183.3 us)
Async XLA Ops:
  10.0 24.8 %collective-permute-start = (bf16[400,384]{1,0:T(8,128)(2,1)}, bf16[400,384]{1,0:T(8,128)(2,1)}, u32[]{:S(2)}, u32[]{:S(2)}) collective-permute-start(bf16[400,384]{1,0:T(8,128)(2,1)} %pad_maximum_fusion.14), channel_id=1, source_target_pairs={{0,1},{1,0},{2,3},{3,2},{4,5},{5,4},{6,7},{7,6},{8,9},{9,8},{10,11... | collective-permute-start | bytes 921608 | tf_op jit(solution)/shard_map/ppermute | solution.py:416
  13.0 24.6 %collective-permute-start.1 = (bf16[400,384]{1,0:T(8,128)(2,1)}, bf16[400,384]{1,0:T(8,128)(2,1)}, u32[]{:S(2)}, u32[]{:S(2)}) collective-permute-start(bf16[400,384]{1,0:T(8,128)(2,1)} %pad_maximum_fusion.14), channel_id=1, source_target_pairs={{0,2},{1,3},{2,0},{3,1},{4,6},{5,7},{6,4},{7,5},{8,10},{9,11},{10,... | collective-permute-start | bytes 921608 | tf_op jit(solution)/shard_map/ppermute | solution.py:416
  15.6 22.0 %collective-permute-start.2 = (bf16[400,384]{1,0:T(8,128)(2,1)}, bf16[400,384]{1,0:T(8,128)(2,1)}, u32[]{:S(2)}, u32[]{:S(2)}) collective-permute-start(bf16[400,384]{1,0:T(8,128)(2,1)} %pad_maximum_fusion.14), channel_id=1, source_target_pairs={{0,3},{1,2},{2,1},{3,0},{4,7},{5,6},{6,5},{7,4},{8,11},{9,10},{10,... | collective-permute-start | bytes 921608 | tf_op jit(solution)/shard_map/ppermute | solution.py:416
  18.7 22.5 %all-to-all-start = ((f32[8,168,192]{2,1,0:T(8,128)}), f32[8,168,192]{2,1,0:T(8,128)S(1)}, u32[]{:S(2)}, u32[]{:S(2)}) async-start(f32[8,168,192]{2,1,0:T(8,128)} %pad_maximum_fusion.3), calls=%async_computation | async-start | bytes 2752512 | tf_op jit(solution)/shard_map/all_to_all | solution.py:458
  47.8 91.6 %all-gather.2.cloned.1.call-start = ((), (), s32[]{:S(2)}) async-start(), calls=%async_computation.8 | async-start | bytes 1671168 | tf_op jit(solution)/shard_map/all_gather | solution.py:623
  49.9 24.5 %collective-permute-start.3 = (bf16[320,768]{1,0:T(8,128)(2,1)}, bf16[320,768]{1,0:T(8,128)(2,1)}, u32[]{:S(2)}, u32[]{:S(2)}) collective-permute-start(bf16[320,768]{1,0:T(8,128)(2,1)} %add_convert_fusion.4), channel_id=1, source_target_pairs={{0,1},{1,0},{2,3},{3,2},{4,5},{5,4},{6,7},{7,6},{8,9},{9,8},{10,11... | collective-permute-start | bytes 1474568 | tf_op jit(solution)/shard_map/ppermute | solution.py:416
  54.5 37.9 %collective-permute-start.4 = (bf16[320,768]{1,0:T(8,128)(2,1)}, bf16[320,768]{1,0:T(8,128)(2,1)}, u32[]{:S(2)}, u32[]{:S(2)}) collective-permute-start(bf16[320,768]{1,0:T(8,128)(2,1)} %add_convert_fusion.4), channel_id=1, source_target_pairs={{0,2},{1,3},{2,0},{3,1},{4,6},{5,7},{6,4},{7,5},{8,10},{9,11},{10,... | collective-permute-start | bytes 1474568 | tf_op jit(solution)/shard_map/ppermute | solution.py:416
  55.5 36.9 %collective-permute-start.5 = (bf16[320,768]{1,0:T(8,128)(2,1)}, bf16[320,768]{1,0:T(8,128)(2,1)}, u32[]{:S(2)}, u32[]{:S(2)}) collective-permute-start(bf16[320,768]{1,0:T(8,128)(2,1)} %add_convert_fusion.4), channel_id=1, source_target_pairs={{0,3},{1,2},{2,1},{3,0},{4,7},{5,6},{6,5},{7,4},{8,11},{9,10},{10,... | collective-permute-start | bytes 1474568 | tf_op jit(solution)/shard_map/ppermute | solution.py:416
  62.9 32.7 %all-to-all-start.2 = ((f32[8,160,192]{2,1,0:T(8,128)}), f32[8,160,192]{2,1,0:T(8,128)S(1)}, u32[]{:S(2)}, u32[]{:S(2)}) async-start(f32[8,160,192]{2,1,0:T(8,128)} %bitcast.362), calls=%async_computation.2 | async-start | bytes 2621440 | tf_op jit(solution)/shard_map/all_to_all | solution.py:458
  105.5 41.1 %collective-permute-start.7 = (bf16[3,1280,128]{2,1,0:T(8,128)(2,1)}, bf16[3,1280,128]{2,1,0:T(8,128)(2,1)}, u32[]{:S(2)}, u32[]{:S(2)}) collective-permute-start(bf16[3,1280,128]{2,1,0:T(8,128)(2,1)} %pad_maximum_fusion.7.rest_0_), channel_id=1, source_target_pairs={{0,4},{4,0},{8,12},{12,8},{1,5},{5,1},{9,13},{13,9},{2,6},{6,2},{1... | collective-permute-start | bytes 2949128 | tf_op jit(solution)/shard_map/ppermute | solution.py:416
  107.7 38.8 %collective-permute-start.8 = (bf16[3,1280,128]{2,1,0:T(8,128)(2,1)}, bf16[3,1280,128]{2,1,0:T(8,128)(2,1)}, u32[]{:S(2)}, u32[]{:S(2)}) collective-permute-start(bf16[3,1280,128]{2,1,0:T(8,128)(2,1)} %pad_maximum_fusion.7.rest_0_), channel_id=1, source_target_pairs={{0,8},{4,12},{8,0},{12,4},{1,9},{5,13},{9,1},{13,5},{2,10},{6,14},... | collective-permute-start | bytes 2949128 | tf_op jit(solution)/shard_map/ppermute | solution.py:416
  109.2 44.6 %collective-permute-start.9 = (bf16[3,1280,128]{2,1,0:T(8,128)(2,1)}, bf16[3,1280,128]{2,1,0:T(8,128)(2,1)}, u32[]{:S(2)}, u32[]{:S(2)}) collective-permute-start(bf16[3,1280,128]{2,1,0:T(8,128)(2,1)} %pad_maximum_fusion.7.rest_0_), channel_id=1, source_target_pairs={{0,12},{4,8},{8,4},{12,0},{1,13},{5,9},{9,5},{13,1},{2,14},{6,10},... | collective-permute-start | bytes 2949128 | tf_op jit(solution)/shard_map/ppermute | solution.py:416
  158.2 60.4 %collective-permute-start.15 = (bf16[384,1536]{1,0:T(8,128)(2,1)}, bf16[384,1536]{1,0:T(8,128)(2,1)}, u32[]{:S(2)}, u32[]{:S(2)}) collective-permute-start(bf16[384,1536]{1,0:T(8,128)(2,1)} %slice.249), channel_id=1, source_target_pairs={{0,4},{4,0},{8,12},{12,8},{1,5},{5,1},{9,13},{13,9},{2,6},{6,2},{1... | collective-permute-start | bytes 3538952 | tf_op jit(solution)/shard_map/ppermute | solution.py:416
  159.6 58.9 %collective-permute-start.16 = (bf16[384,1536]{1,0:T(8,128)(2,1)}, bf16[384,1536]{1,0:T(8,128)(2,1)}, u32[]{:S(2)}, u32[]{:S(2)}) collective-permute-start(bf16[384,1536]{1,0:T(8,128)(2,1)} %slice.249), channel_id=1, source_target_pairs={{0,8},{4,12},{8,0},{12,4},{1,9},{5,13},{9,1},{13,5},{2,10},{6,14},... | collective-permute-start | bytes 3538952 | tf_op jit(solution)/shard_map/ppermute | solution.py:416
  160.2 58.4 %collective-permute-start.17 = (bf16[384,1536]{1,0:T(8,128)(2,1)}, bf16[384,1536]{1,0:T(8,128)(2,1)}, u32[]{:S(2)}, u32[]{:S(2)}) collective-permute-start(bf16[384,1536]{1,0:T(8,128)(2,1)} %slice.249), channel_id=1, source_target_pairs={{0,12},{4,8},{8,4},{12,0},{1,13},{5,9},{9,5},{13,1},{2,14},{6,10},... | collective-permute-start | bytes 3538952 | tf_op jit(solution)/shard_map/ppermute | solution.py:416
  220.7 28.4 %all-to-all-start.3 = ((bf16[4,320,192]{1,2,0:T(8,128)(2,1)}), bf16[4,320,192]{1,2,0:T(8,128)(2,1)S(1)}, u32[]{:S(2)}, u32[]{:S(2)}) async-start(bf16[4,320,192]{1,2,0:T(8,128)(2,1)} %copy.187), calls=%async_computation.3 | async-start | bytes 1179648 | tf_op jit(solution)/shard_map/all_to_all | solution.py:458
  277.0 42.5 %collective-permute-start.21 = (f32[1280,256]{1,0:T(8,128)}, f32[1280,256]{1,0:T(8,128)}, u32[]{:S(2)}, u32[]{:S(2)}) collective-permute-start(f32[1280,256]{1,0:T(8,128)} %get-tuple-element.97.o_own), channel_id=1, source_target_pairs={{0,16},{16,0},{1,17},{17,1},{2,18},{18,2},{3,19},{19,3},{4,20},{20... | collective-permute-start | bytes 3932168 | tf_op jit(solution)/shard_map/ppermute | solution.py:416
  286.7 20.6 %all-to-all-start.4 = ((bf16[4,320,192]{1,2,0:T(8,128)(2,1)}), bf16[4,320,192]{1,2,0:T(8,128)(2,1)S(1)}, u32[]{:S(2)}, u32[]{:S(2)}) async-start(bf16[4,320,192]{1,2,0:T(8,128)(2,1)} %bitcast.179), calls=%async_computation.4 | async-start | bytes 1179648 | tf_op jit(solution)/shard_map/all_to_all | solution.py:458
  312.2 80.8 %collective-permute-start.23 = (bf16[448,1536]{1,0:T(8,128)(2,1)}, bf16[448,1536]{1,0:T(8,128)(2,1)S(1)}, u32[]{:S(2)}, u32[]{:S(2)}) collective-permute-start(bf16[448,1536]{1,0:T(8,128)(2,1)} %get-tuple-element.108), channel_id=1, source_target_pairs={{0,4},{4,0},{8,12},{12,8},{1,5},{5,1},{9,13},{13,9},{2,6},{6,2},{1... | collective-permute-start | bytes 4128776 | tf_op jit(solution)/shard_map/ppermute | solution.py:416
  314.3 78.7 %collective-permute-start.24 = (bf16[448,1536]{1,0:T(8,128)(2,1)}, bf16[448,1536]{1,0:T(8,128)(2,1)}, u32[]{:S(2)}, u32[]{:S(2)}) collective-permute-start(bf16[448,1536]{1,0:T(8,128)(2,1)} %get-tuple-element.109), channel_id=1, source_target_pairs={{0,8},{4,12},{8,0},{12,4},{1,9},{5,13},{9,1},{13,5},{2,10},{6,14},... | collective-permute-start | bytes 4128776 | tf_op jit(solution)/shard_map/ppermute | solution.py:416
  317.3 75.8 %collective-permute-start.25 = (bf16[448,1536]{1,0:T(8,128)(2,1)}, bf16[448,1536]{1,0:T(8,128)(2,1)}, u32[]{:S(2)}, u32[]{:S(2)}) collective-permute-start(bf16[448,1536]{1,0:T(8,128)(2,1)} %get-tuple-element.110), channel_id=1, source_target_pairs={{0,12},{4,8},{8,4},{12,0},{1,13},{5,9},{9,5},{13,1},{2,14},{6,10},... | collective-permute-start | bytes 4128776 | tf_op jit(solution)/shard_map/ppermute | solution.py:416
  393.1 53.2 %all-to-all-start.5 = ((bf16[4,3,1280,128]{3,2,1,0:T(8,128)(2,1)}), bf16[4,3,1280,128]{3,2,1,0:T(8,128)(2,1)}, u32[]{:S(2)}, u32[]{:S(2)}) async-start(bf16[4,3,1280,128]{3,2,1,0:T(8,128)(2,1)} %bitcast.368), calls=%async_computation.5 | async-start | bytes 7864320 | tf_op jit(solution)/shard_map/all_to_all | solution.py:458
  400.9 30.6 %collective-permute-start.26 = (f32[1280,256]{1,0:T(8,128)}, f32[1280,256]{1,0:T(8,128)S(1)}, u32[]{:S(2)}, u32[]{:S(2)}) collective-permute-start(f32[1280,256]{1,0:T(8,128)} %get-tuple-element.113), channel_id=1, source_target_pairs={{0,16},{16,0},{1,17},{17,1},{2,18},{18,2},{3,19},{19,3},{4,20},{20... | collective-permute-start | bytes 3932168 | tf_op jit(solution)/shard_map/ppermute | solution.py:416
  404.0 26.7 %collective-permute-start.28 = (bf16[448,384]{1,0:T(8,128)(2,1)S(1)}, bf16[448,384]{1,0:T(8,128)(2,1)S(1)}, u32[]{:S(2)}, u32[]{:S(2)}) collective-permute-start(bf16[448,384]{1,0:T(8,128)(2,1)S(1)} %get-tuple-element.257), channel_id=1, source_target_pairs={{0,2},{1,3},{2,0},{3,1},{4,6},{5,7},{6,4},{7,5},{8,10},{9,11},{10,... | collective-permute-start | bytes 1032200 | tf_op jit(solution)/shard_map/ppermute | solution.py:416
  406.4 24.3 %collective-permute-start.29 = (bf16[448,384]{1,0:T(8,128)(2,1)S(1)}, bf16[448,384]{1,0:T(8,128)(2,1)S(1)}, u32[]{:S(2)}, u32[]{:S(2)}) collective-permute-start(bf16[448,384]{1,0:T(8,128)(2,1)S(1)} %get-tuple-element.256), channel_id=1, source_target_pairs={{0,3},{1,2},{2,1},{3,0},{4,7},{5,6},{6,5},{7,4},{8,11},{9,10},{10,... | collective-permute-start | bytes 1032200 | tf_op jit(solution)/shard_map/ppermute | solution.py:416
  411.9 20.0 %collective-permute-start.30 = (f32[320,768]{1,0:T(8,128)S(1)}, f32[320,768]{1,0:T(8,128)S(1)}, u32[]{:S(2)}, u32[]{:S(2)}) collective-permute-start(f32[320,768]{1,0:T(8,128)S(1)} %slice.333), channel_id=1, source_target_pairs={{0,16},{16,0},{1,17},{17,1},{2,18},{18,2},{3,19},{19,3},{4,20},{20... | collective-permute-start | bytes 2949128 | tf_op jit(solution)/shard_map/ppermute | solution.py:416
  453.6 59.8 %all-to-all-start.6 = ((bf16[4,320,768]{2,1,0:T(8,128)(2,1)}), bf16[4,320,768]{2,1,0:T(8,128)(2,1)}, u32[]{:S(2)}, u32[]{:S(2)}) async-start(bf16[4,320,768]{2,1,0:T(8,128)(2,1)} %bitcast.377), calls=%async_computation.6 | async-start | bytes 3932160 | tf_op jit(solution)/shard_map/all_to_all | solution.py:458
  466.5 23.7 %collective-permute-start.42 = (f32[4,192]{1,0:T(4,128)S(1)}, f32[4,192]{1,0:T(4,128)S(1)}, u32[]{:S(2)}, u32[]{:S(2)}) collective-permute-start(f32[4,192]{1,0:T(4,128)S(1)} %fusion.46), channel_id=1, source_target_pairs={{0,1},{1,0},{2,3},{3,2},{4,5},{5,4},{6,7},{7,6},{8,9},{9,8},{10,11... | collective-permute-start | bytes 9224 | tf_op jit(solution)/shard_map/ppermute | solution.py:416
  468.6 35.3 %collective-permute-start.43 = (f32[4,192]{1,0:T(4,128)S(1)}, f32[4,192]{1,0:T(4,128)S(1)}, u32[]{:S(2)}, u32[]{:S(2)}) collective-permute-start(f32[4,192]{1,0:T(4,128)S(1)} %fusion.46), channel_id=1, source_target_pairs={{0,2},{1,3},{2,0},{3,1},{4,6},{5,7},{6,4},{7,5},{8,10},{9,11},{10,... | collective-permute-start | bytes 9224 | tf_op jit(solution)/shard_map/ppermute | solution.py:416
  470.9 33.0 %collective-permute-start.44 = (f32[4,192]{1,0:T(4,128)S(1)}, f32[4,192]{1,0:T(4,128)S(1)}, u32[]{:S(2)}, u32[]{:S(2)}) collective-permute-start(f32[4,192]{1,0:T(4,128)S(1)} %fusion.46), channel_id=1, source_target_pairs={{0,3},{1,2},{2,1},{3,0},{4,7},{5,6},{6,5},{7,4},{8,11},{9,10},{10,... | collective-permute-start | bytes 9224 | tf_op jit(solution)/shard_map/ppermute | solution.py:416
  471.9 34.7 %collective-permute-start.34 = (bf16[208,576]{1,0:T(8,128)(2,1)}, bf16[208,576]{1,0:T(8,128)(2,1)S(1)}, u32[]{:S(2)}, u32[]{:S(2)}) collective-permute-start(bf16[208,576]{1,0:T(8,128)(2,1)} %get-tuple-element.264), channel_id=1, source_target_pairs={{0,4},{4,0},{8,12},{12,8},{1,5},{5,1},{9,13},{13,9},{2,6},{6,2},{1... | collective-permute-start | bytes 718856 | tf_op jit(solution)/shard_map/ppermute | solution.py:416
  473.8 32.8 %collective-permute-start.35 = (bf16[208,576]{1,0:T(8,128)(2,1)}, bf16[208,576]{1,0:T(8,128)(2,1)S(1)}, u32[]{:S(2)}, u32[]{:S(2)}) collective-permute-start(bf16[208,576]{1,0:T(8,128)(2,1)} %get-tuple-element.265), channel_id=1, source_target_pairs={{0,8},{4,12},{8,0},{12,4},{1,9},{5,13},{9,1},{13,5},{2,10},{6,14},... | collective-permute-start | bytes 718856 | tf_op jit(solution)/shard_map/ppermute | solution.py:416
  (94 other events, 1021.3 us)
Sparse Core Ops, SparseCore 0:
  58.0 81.3 all-gather.1

commit v2 on v1

--- a/solution.py
+++ b/solution.py
@@ -428,6 +428,15 @@
     return lax.optimization_barrier((value,) + others)[0]
 
 
+def gather_square(value, axis):
+    if lax.axis_size(axis) != 4 or value.shape[1] % 32:
+        return gather(value, axis)
+    half = value.shape[1] // 2
+    near, other = swap(value, axis, 1), swap(value, axis, 2)
+    far = [swap(near[:, :half], axis, 2), swap(other[:, half:], axis, 1)]
+    return [value, near, other, jnp.concatenate(far, axis=1)]
+
+
 def pick(values, index, axis=0):
     return lax.dynamic_index_in_dim(values, index, axis, keepdims=False)
 
@@ -619,12 +628,7 @@
     bias_rows = jnp.pad(up_bias_part, ((0, 13), (0, 0)))
     mlp_low = jnp.concatenate([up_low, down_low, bias_rows], axis=0)
     mlp_cols = jnp.concatenate(gather(mlp_low, "col"), axis=1)
-    proj_full = (
-        lax.all_gather(proj_low, ("row", "col"))
-        .reshape(rows, cols * width, features)
-        .transpose(1, 0, 2)
-        .reshape(cols * width, width_all)
-    )
+    proj_all = lax.all_gather(proj_low, ("row", "col"))
     sent_rows = 2 * features
     up_bias_full = jnp.sum(mlp_cols[sent_rows : sent_rows + 3].astype(jnp.float32), axis=0)
 
@@ -700,12 +704,10 @@
     qkv = low(dot(normed_all, qkv_full) + bias_row)
     kv_own = jnp.stack([qkv[:, h * head_width : (h + 1) * head_width] for h in range(heads)])
     q_own = qkv[:, 2 * width :] * jnp.bfloat16(0.125)
-    core_parts = gather(kv_own, "row")
+    core_parts = gather_square(kv_own, "row")
 
     cot_both = jnp.concatenate(gather(cot_low, "dp"), axis=0)
-    q_own, proj_full, cot_both, core_parts = lax.optimization_barrier(
-        (q_own, proj_full, cot_both, core_parts)
-    )
+    q_own, cot_both, core_parts = lax.optimization_barrier((q_own, cot_both, core_parts))
     parts = [part for held in core_parts for part in gather(held, "dp")]
     q_other = swap(q_own, "dp", 1)
     mlp_got = gather(after(mlp_cols[:sent_rows], *core_parts), "row")
@@ -754,7 +756,12 @@
         order,
         order_rows,
     )
-    attended_low, mlp_got = lax.optimization_barrier((attended_low, mlp_got))
+    attended_low, mlp_got, proj_all = lax.optimization_barrier((attended_low, mlp_got, proj_all))
+    proj_full = (
+        proj_all.reshape(rows, cols * width, features)
+        .transpose(1, 0, 2)
+        .reshape(cols * width, width_all)
+    )
     attended = side_by_side(trade(attended_low.reshape(cols, own, width), "col"))
     out_other = swap(head_out, "dp", 1)
 

time: 567 us -> 547 us (0.965)
  waiting for transfers between devices: 151 us -> 139 us
  starting transfers between devices: 95.4 us -> 89 us
    all_gather x1, waiting for transfers between devices: 30.3 us -> 8.39 us  [shards(): proj_all = lax.all_gather(proj_low, ('row', 'col'))]
    ppermute x46 -> x47, waiting for transfers between devices: 82.1 us -> 100 us  [swap(): lax.ppermute(value, axis, [(source, source ^ step) for source in range(co...]
    all_to_all x8, waiting for transfers between devices: 38.5 us -> 30.4 us  [trade(): return lax.all_to_all(values, axis, 0, 0)]
    all_to_all x8, starting transfers between devices: 44.4 us -> 37.6 us  [trade(): return lax.all_to_all(values, axis, 0, 0)]
    unnamed x151 -> x153, local copies, waits for them, and re-layouts: 13.9 us -> 14.2 us
    ppermute x46 -> x47, starting transfers between devices: 51 us -> 51.3 us  [swap(): lax.ppermute(value, axis, [(source, source ^ step) for source in range(co...]
  transfers between devices with their start and end apart: 55 -> 56, of which waited for: 17 -> 19; matrix products, arithmetic and copies ran while one was open for 22% -> 21% of each run, Pallas kernels for 23% -> 24%
where the time goes in v2:
time: 547 us; the launch traced here: 542 us
  waiting for transfers between devices  139 us (25%)
  Pallas kernels  131 us (24%)
  starting transfers between devices  89 us (16%)
  local copies, waits for them, and re-layouts  78.2 us (14%)
  other arithmetic  50.1 us (9%)
  matrix products  38.9 us (7%)
  between operations  16 us (3%)
    ppermute x47, waiting for transfers between devices, swap(): lax.ppermute(value, axis, [(source, source ^ step) for source in range(co...  100 us
    pallas_call x1, Pallas kernels, attend_backward(): pl.pallas_call(functools.partial(backward_kernel, heads, part_count, rows...  73.5 us
    pallas_call x1, Pallas kernels, attend_forward(): pl.pallas_call(functools.partial(forward_kernel, heads, part_count, rows,...  57.5 us
    ppermute x47, starting transfers between devices, swap(): lax.ppermute(value, axis, [(source, source ^ step) for source in range(co...  51.3 us
    dot_general x12, matrix products, dot(): lax.dot_general(left, right, (((left_dim,), (right_dim,)), ((), ())), pre...  38.9 us
    all_to_all x8, starting transfers between devices, trade(): return lax.all_to_all(values, axis, 0, 0)  37.6 us
    all_to_all x8, waiting for transfers between devices, trade(): return lax.all_to_all(values, axis, 0, 0)  30.4 us
    unnamed x153, local copies, waits for them, and re-layouts  14.2 us
  transfers between devices with their start and end apart: 56, of which 19 were waited for; matrix products, arithmetic and copies ran while one was open for 21% of the time, Pallas kernels for 24%

profile of v2, /device:TPU:0, one launch (start us, length us, event | category | flops | bytes accessed | tf_op | source)
XLA Modules:
  0.0 542.3 jit_solution(12720872860532819057)
XLA Ops:
  18.7 4.1 all-to-all-start
  44.1 3.6 all-to-all-start.1
  49.8 4.6 collective-permute-start.3
  57.0 4.4 all-to-all-done.1
  63.0 3.6 all-to-all-start.2
  67.1 6.6 %collective-permute-done.3 = bf16[320,768]{1,0:T(8,128)(2,1)} collective-permute-done((bf16[320,768]{1,0:T(8,128)(2,1)}, bf16[320,768]{1,0:T(8,128)(2,1)}, u32[]{:S(2)}, u32[]{:S(2)}) %collective-permute-start.3) | collective-permute-done | bytes 491552 | tf_op jit(solution)/shard_map/ppermute | solution.py:416
  73.7 17.2 %collective-permute-done.4 = bf16[320,768]{1,0:T(8,128)(2,1)} collective-permute-done((bf16[320,768]{1,0:T(8,128)(2,1)}, bf16[320,768]{1,0:T(8,128)(2,1)}, u32[]{:S(2)}, u32[]{:S(2)}) %collective-permute-start.4) | collective-permute-done | bytes 491552 | tf_op jit(solution)/shard_map/ppermute | solution.py:416
  98.5 3.4 fusion.7
  106.6 15.9 %collective-permute-done.8.rest_4_.rest_2_ = bf16[3,1280,128]{2,1,0:T(8,128)(2,1)} collective-permute-done((bf16[3,1280,128]{2,1,0:T(8,128)(2,1)}, bf16[3,1280,128]{2,1,0:T(8,128)(2,1)}, u32[]{:S(2)}, u32[]{:S(2)}) %collective-permute-start.8) | collective-permute-done | bytes 983072 | tf_op jit(solution)/shard_map/ppermute | solution.py:416
  133.2 3.1 collective-permute-done.9
  146.5 57.5 %shard_map.263 = (f32[1280,256]{1,0:T(8,128)}, bf16[1280,192]{1,0:T(8,128)(2,1)}) custom-call(s32[5,2]{1,0:T(8,128)} %copy.183.cnt, s32[5,20]{1,0:T(8,128)} %select_reduce_fusion.2.lst, s32[64]{0:T(128)} %stack.540.offs, bf16[1280,192]{1,0:T(8,128)(2,1)} %slice_multiply_fusion.q_ref.q_own, s32[1,10240]{1,0:T(1,128)} %bitcast.392, ...), custom_call_target="tpu_custom_call" | custom-call | flops 80530636800 | bytes 15728640 | tf_op jit(solution)/shard_map/pallas_call | solution.py:227
  204.0 8.4 %all-gather.2.cloned.1.call-done = bf16[16,192,192]{2,1,0:T(8,128)(2,1)} async-done(((bf16[1,192,192]{2,1,0:T(8,128)(2,1)}), bf16[16,192,192]{2,1,0:T(8,128)(2,1)}) %all-gather.2.cloned.1.call-update) | async-done | bytes 1179664 | tf_op jit(solution)/shard_map/all_gather | solution.py:631
  215.0 5.3 all-to-all-start.3
  227.7 3.6 copy.215
  241.0 3.4 fusion.69
  244.4 7.4 %multiply_convert_fusion = (bf16[640,1536]{1,0:T(8,128)(2,1)}, bf16[640,1536]{1,0:T(8,128)(2,1)S(1)}) fusion(f32[1536]{0:T(1024)S(1)} %copy-done.57, f32[640,1536]{1,0:T(8,128)S(1)} %fusion.69, bf16[768,1536]{1,0:T(8,128)(2,1)} %bitcast.177, bf16[320,768]{1,0:T(8,128)(2,1)S(1)} %collective-permute-done.19, bf16[320,768]{1,0:T(8,128)(2,1)S(1)} %add_convert_fusion.3), kind=kOutput, calls=%fused_computation.11 | convolution fusion | flops 1534525440 | bytes 11212800 | tf_op jit(solution)/shard_map/dot_general | solution.py:461
  251.9 4.1 fusion.70
  271.8 5.5 %all-to-all-start.4 = ((bf16[4,320,192]{1,2,0:T(8,128)(2,1)}), bf16[4,320,192]{1,2,0:T(8,128)(2,1)S(1)}, u32[]{:S(2)}, u32[]{:S(2)}) async-start(bf16[4,320,192]{1,2,0:T(8,128)(2,1)} %bitcast.179), calls=%async_computation.4 | async-start | bytes 1179648 | tf_op jit(solution)/shard_map/all_to_all | solution.py:467
  277.4 3.9 convolution_convert_fusion.1
  294.8 3.6 fusion.12
  304.1 73.5 %shard_map.264 = (f32[1280,256]{1,0:T(8,128)}, f32[1280,256]{1,0:T(8,128)}, bf16[4,3,4,2,160,128]{5,4,3,2,1,0:T(8,128)(2,1)}) custom-call(s32[10,2]{1,0:T(8,128)} %copy.192.cnt, s32[10,10]{1,0:T(8,128)} %select_reduce_fusion.1.lst, s32[32]{0:T(128)} %stack.465.offs, bf16[1280,192]{1,0:T(8,128)(2,1)} %slice_multiply_fusion.q_ref.q_own, ...), custom_call_target="tpu_custom_call" | custom-call | flops 100663296000 | bytes 7864320 | tf_op jit(solution)/shard_map/pallas_call | solution.py:370
  377.6 7.3 %all-to-all-start.5 = ((bf16[4,3,1280,128]{3,2,1,0:T(8,128)(2,1)}), bf16[4,3,1280,128]{3,2,1,0:T(8,128)(2,1)}, u32[]{:S(2)}, u32[]{:S(2)}) async-start(bf16[4,3,1280,128]{3,2,1,0:T(8,128)(2,1)} %bitcast.368), calls=%async_computation.5 | async-start | bytes 7864320 | tf_op jit(solution)/shard_map/all_to_all | solution.py:467
  385.0 3.6 collective-permute-start.27
  395.6 3.4 fusion.71
  400.2 7.6 %collective-permute-done.28 = bf16[448,384]{1,0:T(8,128)(2,1)S(1)} collective-permute-done((bf16[448,384]{1,0:T(8,128)(2,1)S(1)}, bf16[448,384]{1,0:T(8,128)(2,1)S(1)}, u32[]{:S(2)}, u32[]{:S(2)}) %collective-permute-start.28) | collective-permute-done | bytes 344096 | tf_op jit(solution)/shard_map/ppermute | solution.py:416
  407.9 10.2 %collective-permute-done.29 = bf16[448,384]{1,0:T(8,128)(2,1)S(1)} collective-permute-done((bf16[448,384]{1,0:T(8,128)(2,1)S(1)}, bf16[448,384]{1,0:T(8,128)(2,1)S(1)}, u32[]{:S(2)}, u32[]{:S(2)}) %collective-permute-start.29) | collective-permute-done | bytes 344096 | tf_op jit(solution)/shard_map/ppermute | solution.py:416
  421.9 9.8 %all-to-all-done.5 = bf16[4,3,1280,128]{3,2,1,0:T(8,128)(2,1)} async-done(((bf16[4,3,1280,128]{3,2,1,0:T(8,128)(2,1)}), bf16[4,3,1280,128]{3,2,1,0:T(8,128)(2,1)}, u32[]{:S(2)}, u32[]{:S(2)}) %all-to-all-start.5) | async-done | bytes 3932192 | tf_op jit(solution)/shard_map/all_to_all | solution.py:467
  438.9 4.6 all-to-all-start.6
  457.9 18.6 %collective-permute-done.43 = f32[4,192]{1,0:T(4,128)S(1)} collective-permute-done((f32[4,192]{1,0:T(4,128)S(1)}, f32[4,192]{1,0:T(4,128)S(1)}, u32[]{:S(2)}, u32[]{:S(2)}) %collective-permute-start.43) | collective-permute-done | bytes 3104 | tf_op jit(solution)/shard_map/ppermute | solution.py:416
  476.9 13.2 %collective-permute-done.44 = f32[4,192]{1,0:T(4,128)S(1)} collective-permute-done((f32[4,192]{1,0:T(4,128)S(1)}, f32[4,192]{1,0:T(4,128)S(1)}, u32[]{:S(2)}, u32[]{:S(2)}) %collective-permute-start.44) | collective-permute-done | bytes 3104 | tf_op jit(solution)/shard_map/ppermute | solution.py:416
  505.8 3.6 all-to-all-start.7
  511.4 13.1 %all-to-all-done.7 = bf16[8,176,384]{2,1,0:T(8,128)(2,1)S(1)} async-done(((bf16[8,176,384]{2,1,0:T(8,128)(2,1)}), bf16[8,176,384]{2,1,0:T(8,128)(2,1)S(1)}, u32[]{:S(2)}, u32[]{:S(2)}) %all-to-all-start.7) | async-done | bytes 1081376 | tf_op jit(solution)/shard_map/all_to_all | solution.py:467
  (477 shorter events, 188.7 us)
Async XLA Ops:
  10.0 24.8 %collective-permute-start = (bf16[400,384]{1,0:T(8,128)(2,1)}, bf16[400,384]{1,0:T(8,128)(2,1)}, u32[]{:S(2)}, u32[]{:S(2)}) collective-permute-start(bf16[400,384]{1,0:T(8,128)(2,1)} %pad_maximum_fusion.15), channel_id=1, source_target_pairs={{0,1},{1,0},{2,3},{3,2},{4,5},{5,4},{6,7},{7,6},{8,9},{9,8},{10,11... | collective-permute-start | bytes 921608 | tf_op jit(solution)/shard_map/ppermute | solution.py:416
  13.0 24.6 %collective-permute-start.1 = (bf16[400,384]{1,0:T(8,128)(2,1)}, bf16[400,384]{1,0:T(8,128)(2,1)}, u32[]{:S(2)}, u32[]{:S(2)}) collective-permute-start(bf16[400,384]{1,0:T(8,128)(2,1)} %pad_maximum_fusion.15), channel_id=1, source_target_pairs={{0,2},{1,3},{2,0},{3,1},{4,6},{5,7},{6,4},{7,5},{8,10},{9,11},{10,... | collective-permute-start | bytes 921608 | tf_op jit(solution)/shard_map/ppermute | solution.py:416
  15.6 22.0 %collective-permute-start.2 = (bf16[400,384]{1,0:T(8,128)(2,1)}, bf16[400,384]{1,0:T(8,128)(2,1)}, u32[]{:S(2)}, u32[]{:S(2)}) collective-permute-start(bf16[400,384]{1,0:T(8,128)(2,1)} %pad_maximum_fusion.15), channel_id=1, source_target_pairs={{0,3},{1,2},{2,1},{3,0},{4,7},{5,6},{6,5},{7,4},{8,11},{9,10},{10,... | collective-permute-start | bytes 921608 | tf_op jit(solution)/shard_map/ppermute | solution.py:416
  18.7 22.5 %all-to-all-start = ((f32[8,168,192]{2,1,0:T(8,128)}), f32[8,168,192]{2,1,0:T(8,128)S(1)}, u32[]{:S(2)}, u32[]{:S(2)}) async-start(f32[8,168,192]{2,1,0:T(8,128)} %pad_maximum_fusion.3), calls=%async_computation | async-start | bytes 2752512 | tf_op jit(solution)/shard_map/all_to_all | solution.py:467
  49.8 23.9 %collective-permute-start.3 = (bf16[320,768]{1,0:T(8,128)(2,1)}, bf16[320,768]{1,0:T(8,128)(2,1)}, u32[]{:S(2)}, u32[]{:S(2)}) collective-permute-start(bf16[320,768]{1,0:T(8,128)(2,1)} %add_convert_fusion.4), channel_id=1, source_target_pairs={{0,1},{1,0},{2,3},{3,2},{4,5},{5,4},{6,7},{7,6},{8,9},{9,8},{10,11... | collective-permute-start | bytes 1474568 | tf_op jit(solution)/shard_map/ppermute | solution.py:416
  54.4 36.4 %collective-permute-start.4 = (bf16[320,768]{1,0:T(8,128)(2,1)}, bf16[320,768]{1,0:T(8,128)(2,1)}, u32[]{:S(2)}, u32[]{:S(2)}) collective-permute-start(bf16[320,768]{1,0:T(8,128)(2,1)} %add_convert_fusion.4), channel_id=1, source_target_pairs={{0,2},{1,3},{2,0},{3,1},{4,6},{5,7},{6,4},{7,5},{8,10},{9,11},{10,... | collective-permute-start | bytes 1474568 | tf_op jit(solution)/shard_map/ppermute | solution.py:416
  55.4 35.4 %collective-permute-start.5 = (bf16[320,768]{1,0:T(8,128)(2,1)}, bf16[320,768]{1,0:T(8,128)(2,1)}, u32[]{:S(2)}, u32[]{:S(2)}) collective-permute-start(bf16[320,768]{1,0:T(8,128)(2,1)} %add_convert_fusion.4), channel_id=1, source_target_pairs={{0,3},{1,2},{2,1},{3,0},{4,7},{5,6},{6,5},{7,4},{8,11},{9,10},{10,... | collective-permute-start | bytes 1474568 | tf_op jit(solution)/shard_map/ppermute | solution.py:416
  63.0 31.2 %all-to-all-start.2 = ((f32[8,160,192]{2,1,0:T(8,128)}), f32[8,160,192]{2,1,0:T(8,128)S(1)}, u32[]{:S(2)}, u32[]{:S(2)}) async-start(f32[8,160,192]{2,1,0:T(8,128)} %bitcast.362), calls=%async_computation.2 | async-start | bytes 2621440 | tf_op jit(solution)/shard_map/all_to_all | solution.py:467
  66.5 145.8 %all-gather.2.cloned.1.call-start = ((), (), s32[]{:S(2)}) async-start(), calls=%async_computation.8 | async-start | bytes 1671168 | tf_op jit(solution)/shard_map/all_gather | solution.py:631
  103.1 19.4 %collective-permute-start.8 = (bf16[3,1280,128]{2,1,0:T(8,128)(2,1)}, bf16[3,1280,128]{2,1,0:T(8,128)(2,1)}, u32[]{:S(2)}, u32[]{:S(2)}) collective-permute-start(bf16[3,1280,128]{2,1,0:T(8,128)(2,1)} %pad_maximum_fusion.7.rest_0_), channel_id=1, source_target_pairs={{0,8},{4,12},{8,0},{12,4},{1,9},{5,13},{9,1},{13,5},{2,10},{6,14},... | collective-permute-start | bytes 2949128 | tf_op jit(solution)/shard_map/ppermute | solution.py:416
  105.1 21.2 %collective-permute-start.7 = (bf16[3,1280,128]{2,1,0:T(8,128)(2,1)}, bf16[3,1280,128]{2,1,0:T(8,128)(2,1)}, u32[]{:S(2)}, u32[]{:S(2)}) collective-permute-start(bf16[3,1280,128]{2,1,0:T(8,128)(2,1)} %pad_maximum_fusion.7.rest_0_), channel_id=1, source_target_pairs={{0,4},{4,0},{8,12},{12,8},{1,5},{5,1},{9,13},{13,9},{2,6},{6,2},{1... | collective-permute-start | bytes 2949128 | tf_op jit(solution)/shard_map/ppermute | solution.py:416
  106.6 22.8 %collective-permute-start.6 = (bf16[320,768]{1,0:T(8,128)(2,1)S(1)}, bf16[320,768]{1,0:T(8,128)(2,1)S(1)}, u32[]{:S(2)}, u32[]{:S(2)}) collective-permute-start(bf16[320,768]{1,0:T(8,128)(2,1)S(1)} %convert_element_type.293), channel_id=1, source_target_pairs={{0,16},{16,0},{1,17},{17,1},{2,18},{18,2},{3,19},{19,3},{4,20},{20... | collective-permute-start | bytes 1474568 | tf_op jit(solution)/shard_map/ppermute | solution.py:416
  142.7 69.6 %collective-permute-start.16 = (bf16[384,1536]{1,0:T(8,128)(2,1)}, bf16[384,1536]{1,0:T(8,128)(2,1)}, u32[]{:S(2)}, u32[]{:S(2)}) collective-permute-start(bf16[384,1536]{1,0:T(8,128)(2,1)} %slice.257), channel_id=1, source_target_pairs={{0,4},{4,0},{8,12},{12,8},{1,5},{5,1},{9,13},{13,9},{2,6},{6,2},{1... | collective-permute-start | bytes 3538952 | tf_op jit(solution)/shard_map/ppermute | solution.py:416
  144.9 67.4 %collective-permute-start.17 = (bf16[384,1536]{1,0:T(8,128)(2,1)}, bf16[384,1536]{1,0:T(8,128)(2,1)}, u32[]{:S(2)}, u32[]{:S(2)}) collective-permute-start(bf16[384,1536]{1,0:T(8,128)(2,1)} %slice.257), channel_id=1, source_target_pairs={{0,8},{4,12},{8,0},{12,4},{1,9},{5,13},{9,1},{13,5},{2,10},{6,14},... | collective-permute-start | bytes 3538952 | tf_op jit(solution)/shard_map/ppermute | solution.py:416
  145.0 67.4 %collective-permute-start.18 = (bf16[384,1536]{1,0:T(8,128)(2,1)}, bf16[384,1536]{1,0:T(8,128)(2,1)S(1)}, u32[]{:S(2)}, u32[]{:S(2)}) collective-permute-start(bf16[384,1536]{1,0:T(8,128)(2,1)} %slice.257), channel_id=1, source_target_pairs={{0,12},{4,8},{8,4},{12,0},{1,13},{5,9},{9,5},{13,1},{2,14},{6,10},... | collective-permute-start | bytes 3538952 | tf_op jit(solution)/shard_map/ppermute | solution.py:416
  215.0 21.1 %all-to-all-start.3 = ((bf16[4,320,192]{1,2,0:T(8,128)(2,1)}), bf16[4,320,192]{1,2,0:T(8,128)(2,1)S(1)}, u32[]{:S(2)}, u32[]{:S(2)}) async-start(bf16[4,320,192]{1,2,0:T(8,128)(2,1)} %copy.185), calls=%async_computation.3 | async-start | bytes 1179648 | tf_op jit(solution)/shard_map/all_to_all | solution.py:467
  262.1 42.0 %collective-permute-start.22 = (f32[1280,256]{1,0:T(8,128)}, f32[1280,256]{1,0:T(8,128)}, u32[]{:S(2)}, u32[]{:S(2)}) collective-permute-start(f32[1280,256]{1,0:T(8,128)} %get-tuple-element.97.o_own), channel_id=1, source_target_pairs={{0,16},{16,0},{1,17},{17,1},{2,18},{18,2},{3,19},{19,3},{4,20},{20... | collective-permute-start | bytes 3932168 | tf_op jit(solution)/shard_map/ppermute | solution.py:416
  271.8 21.7 %all-to-all-start.4 = ((bf16[4,320,192]{1,2,0:T(8,128)(2,1)}), bf16[4,320,192]{1,2,0:T(8,128)(2,1)S(1)}, u32[]{:S(2)}, u32[]{:S(2)}) async-start(bf16[4,320,192]{1,2,0:T(8,128)(2,1)} %bitcast.179), calls=%async_computation.4 | async-start | bytes 1179648 | tf_op jit(solution)/shard_map/all_to_all | solution.py:467
  298.4 79.1 %collective-permute-start.24 = (bf16[448,1536]{1,0:T(8,128)(2,1)}, bf16[448,1536]{1,0:T(8,128)(2,1)S(1)}, u32[]{:S(2)}, u32[]{:S(2)}) collective-permute-start(bf16[448,1536]{1,0:T(8,128)(2,1)} %get-tuple-element.108), channel_id=1, source_target_pairs={{0,4},{4,0},{8,12},{12,8},{1,5},{5,1},{9,13},{13,9},{2,6},{6,2},{1... | collective-permute-start | bytes 4128776 | tf_op jit(solution)/shard_map/ppermute | solution.py:416
  299.5 78.0 %collective-permute-start.25 = (bf16[448,1536]{1,0:T(8,128)(2,1)}, bf16[448,1536]{1,0:T(8,128)(2,1)}, u32[]{:S(2)}, u32[]{:S(2)}) collective-permute-start(bf16[448,1536]{1,0:T(8,128)(2,1)} %get-tuple-element.109), channel_id=1, source_target_pairs={{0,8},{4,12},{8,0},{12,4},{1,9},{5,13},{9,1},{13,5},{2,10},{6,14},... | collective-permute-start | bytes 4128776 | tf_op jit(solution)/shard_map/ppermute | solution.py:416
  300.3 77.3 %collective-permute-start.26 = (bf16[448,1536]{1,0:T(8,128)(2,1)}, bf16[448,1536]{1,0:T(8,128)(2,1)}, u32[]{:S(2)}, u32[]{:S(2)}) collective-permute-start(bf16[448,1536]{1,0:T(8,128)(2,1)} %get-tuple-element.110), channel_id=1, source_target_pairs={{0,12},{4,8},{8,4},{12,0},{1,13},{5,9},{9,5},{13,1},{2,14},{6,10},... | collective-permute-start | bytes 4128776 | tf_op jit(solution)/shard_map/ppermute | solution.py:416
  377.6 54.1 %all-to-all-start.5 = ((bf16[4,3,1280,128]{3,2,1,0:T(8,128)(2,1)}), bf16[4,3,1280,128]{3,2,1,0:T(8,128)(2,1)}, u32[]{:S(2)}, u32[]{:S(2)}) async-start(bf16[4,3,1280,128]{3,2,1,0:T(8,128)(2,1)} %bitcast.368), calls=%async_computation.5 | async-start | bytes 7864320 | tf_op jit(solution)/shard_map/all_to_all | solution.py:467
  385.0 33.9 %collective-permute-start.27 = (f32[1280,256]{1,0:T(8,128)}, f32[1280,256]{1,0:T(8,128)S(1)}, u32[]{:S(2)}, u32[]{:S(2)}) collective-permute-start(f32[1280,256]{1,0:T(8,128)} %get-tuple-element.113), channel_id=1, source_target_pairs={{0,16},{16,0},{1,17},{17,1},{2,18},{18,2},{3,19},{19,3},{4,20},{20... | collective-permute-start | bytes 3932168 | tf_op jit(solution)/shard_map/ppermute | solution.py:416
  391.4 26.6 %collective-permute-start.29 = (bf16[448,384]{1,0:T(8,128)(2,1)S(1)}, bf16[448,384]{1,0:T(8,128)(2,1)S(1)}, u32[]{:S(2)}, u32[]{:S(2)}) collective-permute-start(bf16[448,384]{1,0:T(8,128)(2,1)S(1)} %get-tuple-element.257), channel_id=1, source_target_pairs={{0,2},{1,3},{2,0},{3,1},{4,6},{5,7},{6,4},{7,5},{8,10},{9,11},{10,... | collective-permute-start | bytes 1032200 | tf_op jit(solution)/shard_map/ppermute | solution.py:416
  393.8 24.2 %collective-permute-start.30 = (bf16[448,384]{1,0:T(8,128)(2,1)S(1)}, bf16[448,384]{1,0:T(8,128)(2,1)S(1)}, u32[]{:S(2)}, u32[]{:S(2)}) collective-permute-start(bf16[448,384]{1,0:T(8,128)(2,1)S(1)} %get-tuple-element.256), channel_id=1, source_target_pairs={{0,3},{1,2},{2,1},{3,0},{4,7},{5,6},{6,5},{7,4},{8,11},{9,10},{10,... | collective-permute-start | bytes 1032200 | tf_op jit(solution)/shard_map/ppermute | solution.py:416
  399.1 20.1 %collective-permute-start.31 = (f32[320,768]{1,0:T(8,128)S(1)}, f32[320,768]{1,0:T(8,128)S(1)}, u32[]{:S(2)}, u32[]{:S(2)}) collective-permute-start(f32[320,768]{1,0:T(8,128)S(1)} %slice.343), channel_id=1, source_target_pairs={{0,16},{16,0},{1,17},{17,1},{2,18},{18,2},{3,19},{19,3},{4,20},{20... | collective-permute-start | bytes 2949128 | tf_op jit(solution)/shard_map/ppermute | solution.py:416
  438.9 60.7 %all-to-all-start.6 = ((bf16[4,320,768]{2,1,0:T(8,128)(2,1)}), bf16[4,320,768]{2,1,0:T(8,128)(2,1)}, u32[]{:S(2)}, u32[]{:S(2)}) async-start(bf16[4,320,768]{2,1,0:T(8,128)(2,1)} %bitcast.377), calls=%async_computation.6 | async-start | bytes 3932160 | tf_op jit(solution)/shard_map/all_to_all | solution.py:467
  451.1 25.3 %collective-permute-start.43 = (f32[4,192]{1,0:T(4,128)S(1)}, f32[4,192]{1,0:T(4,128)S(1)}, u32[]{:S(2)}, u32[]{:S(2)}) collective-permute-start(f32[4,192]{1,0:T(4,128)S(1)} %fusion.46), channel_id=1, source_target_pairs={{0,1},{1,0},{2,3},{3,2},{4,5},{5,4},{6,7},{7,6},{8,9},{9,8},{10,11... | collective-permute-start | bytes 9224 | tf_op jit(solution)/shard_map/ppermute | solution.py:416
  453.2 36.9 %collective-permute-start.44 = (f32[4,192]{1,0:T(4,128)S(1)}, f32[4,192]{1,0:T(4,128)S(1)}, u32[]{:S(2)}, u32[]{:S(2)}) collective-permute-start(f32[4,192]{1,0:T(4,128)S(1)} %fusion.46), channel_id=1, source_target_pairs={{0,2},{1,3},{2,0},{3,1},{4,6},{5,7},{6,4},{7,5},{8,10},{9,11},{10,... | collective-permute-start | bytes 9224 | tf_op jit(solution)/shard_map/ppermute | solution.py:416
  455.6 34.6 %collective-permute-start.45 = (f32[4,192]{1,0:T(4,128)S(1)}, f32[4,192]{1,0:T(4,128)S(1)}, u32[]{:S(2)}, u32[]{:S(2)}) collective-permute-start(f32[4,192]{1,0:T(4,128)S(1)} %fusion.46), channel_id=1, source_target_pairs={{0,3},{1,2},{2,1},{3,0},{4,7},{5,6},{6,5},{7,4},{8,11},{9,10},{10,... | collective-permute-start | bytes 9224 | tf_op jit(solution)/shard_map/ppermute | solution.py:416
  456.5 36.3 %collective-permute-start.35 = (bf16[208,576]{1,0:T(8,128)(2,1)}, bf16[208,576]{1,0:T(8,128)(2,1)S(1)}, u32[]{:S(2)}, u32[]{:S(2)}) collective-permute-start(bf16[208,576]{1,0:T(8,128)(2,1)} %get-tuple-element.264), channel_id=1, source_target_pairs={{0,4},{4,0},{8,12},{12,8},{1,5},{5,1},{9,13},{13,9},{2,6},{6,2},{1... | collective-permute-start | bytes 718856 | tf_op jit(solution)/shard_map/ppermute | solution.py:416
  456.9 35.9 %collective-permute-start.36 = (bf16[208,576]{1,0:T(8,128)(2,1)}, bf16[208,576]{1,0:T(8,128)(2,1)S(1)}, u32[]{:S(2)}, u32[]{:S(2)}) collective-permute-start(bf16[208,576]{1,0:T(8,128)(2,1)} %get-tuple-element.265), channel_id=1, source_target_pairs={{0,8},{4,12},{8,0},{12,4},{1,9},{5,13},{9,1},{13,5},{2,10},{6,14},... | collective-permute-start | bytes 718856 | tf_op jit(solution)/shard_map/ppermute | solution.py:416
  (96 other events, 1046.9 us)
Sparse Core Ops, SparseCore 0:
  139.5 72.8 all-gather.1
